TPU v7x, 32 devices: a whole 2x2x4 slice. The times are simulated.
32 devices in a mesh: seq: 8 (over z, x), batch: 4 (over y, core).
Axes of the slice: x: 2, y: 2, z: 4, core: 2. Of those that a mesh axis runs over, the one named last changes fastest.
Arguments:
- tokens: bfloat16 [4, 4096, 576], P('batch', 'seq'), may hold values from -6 to 6
- segment_ids: int32 [4, 4096], P('batch', 'seq'), may hold values from 0 to 130, as said below
- gain_attn: bfloat16 [576], replicated, may hold values from 0.5 to 1.5
- w_query: bfloat16 [576, 576], replicated, may hold values from -0.5 to 0.5
- w_key: bfloat16 [576, 192], replicated, may hold values from -0.25 to 0.25
- w_value: bfloat16 [576, 192], replicated, may hold values from -0.25 to 0.25
- w_out: bfloat16 [576, 576], replicated, may hold values from -2 to 2
- gain_mlp: bfloat16 [576], replicated, may hold values from 0.5 to 1.5
- w_gate: bfloat16 [576, 1536], replicated, may hold values from -0.25 to 0.25
- w_up: bfloat16 [576, 1536], replicated, may hold values from -0.25 to 0.25
- w_down: bfloat16 [1536, 576], replicated, may hold values from -0.15625 to 0.15625
- cotangent: bfloat16 [4, 4096, 576], P('batch', 'seq'), may hold values from -6 to 6
Outputs:
- output: bfloat16 [4, 4096, 576], P('batch', 'seq')
- tokens_grad: float32 [4, 4096, 576], P('batch', 'seq')
- gain_attn_grad: float32 [576], replicated
- w_query_grad: float32 [576, 576], replicated
- w_key_grad: float32 [576, 192], replicated
- w_value_grad: float32 [576, 192], replicated
- w_out_grad: float32 [576, 576], replicated
- gain_mlp_grad: float32 [576], replicated
- w_gate_grad: float32 [576, 1536], replicated
- w_up_grad: float32 [576, 1536], replicated
- w_down_grad: float32 [1536, 576], replicated
Inputs may be any that keep to these rules, and one draw needn't show every extreme that they name: `segment_ids`: along each sequence the ids start at 0, never fall and rise by at most one from token to token; each sequence holds exactly 131 documents; one document of each sequence begins within its first 512 tokens and ends within its last 512.
All inputs are finite; a program needn't handle non-finite values.
Results may differ from a plain program's by a relative error of at most 0.02.
Values may be sent and summed in bfloat16 or wider, within the bound.
A program may use at most 192 MiB of HBM per device.

v0:
```python
import jax
import jax.numpy as jnp
from jax import lax
from jax.sharding import PartitionSpec as P

H = 9
KVH = 3
HD = 64


epsilon = 1e-05
theta_base = 10000.0
masked_value = -1e30


def positions(seg_ids):
    length = seg_ids.shape[0]
    index = jnp.arange(length, dtype=jnp.int32)
    fresh = jnp.concatenate([jnp.ones((1,), dtype=jnp.bool_), seg_ids[1:] != seg_ids[:-1]])
    begins = lax.cummax(jnp.where(fresh, index, jnp.zeros_like(index)), axis=0)
    return index - begins


def rotate(vectors, places):
    half = vectors.shape[-1] // 2
    freqs = theta_base ** (-2.0 * jnp.arange(half, dtype=jnp.float32) / vectors.shape[-1])
    angles = places.astype(jnp.float32)[:, None] * freqs[None, :]
    cosine = jnp.cos(angles)[:, None, :]
    sine = jnp.sin(angles)[:, None, :]
    first = vectors[..., :half]
    second = vectors[..., half:]
    return jnp.concatenate(
        [first * cosine - second * sine, second * cosine + first * sine], axis=-1
    )


def contract_rows(left, right):
    return lax.dot_general(
        left, right, (((0,), (0,)), ((), ())), preferred_element_type=jnp.float32
    )


def times_transposed(left, weight):
    return lax.dot_general(
        left, weight, (((1,), (1,)), ((), ())), preferred_element_type=jnp.float32
    )


def block_size(total_count):
    chosen = total_count
    for option in (512, 1024):
        chosen = option
    return chosen


def local(
    tokens,
    segment_ids,
    gain_attn,
    w_query,
    w_key,
    w_value,
    w_out,
    gain_mlp,
    w_gate,
    w_up,
    w_down,
    cotangent,
):
    seq_rank = lax.axis_index("seq")
    local_rows = tokens.shape[1]
    group_size = H // KVH
    kv_width = KVH * HD
    factor = HD ** (-0.5)
    inputs = tokens[0].astype(jnp.float32)
    cot_rows = cotangent[0]
    local_seg = segment_ids[0]
    all_seg = lax.all_gather(local_seg, "seq", axis=0, tiled=True)
    offset = seq_rank * local_rows
    local_pos = lax.dynamic_slice_in_dim(positions(all_seg), offset, local_rows)
    query_index = offset + jnp.arange(local_rows, dtype=jnp.int32)
    inv_first = lax.rsqrt(jnp.mean(inputs * inputs, axis=-1, keepdims=True) + epsilon)
    scaled_first = inputs * inv_first
    gain_first = gain_attn.astype(jnp.float32)
    normed = (scaled_first * gain_first).astype(jnp.bfloat16)
    queries = rotate(
        jnp.dot(normed, w_query, preferred_element_type=jnp.float32).reshape(local_rows, H, HD),
        local_pos,
    )
    queries = queries.astype(jnp.bfloat16).reshape(local_rows, KVH, group_size, HD)
    keys_rot = rotate(
        jnp.dot(normed, w_key, preferred_element_type=jnp.float32).reshape(local_rows, KVH, HD),
        local_pos,
    )
    keys_rot = keys_rot.astype(jnp.bfloat16)
    values_local = jnp.dot(normed, w_value, preferred_element_type=jnp.float32).astype(jnp.bfloat16)
    packed = jnp.concatenate([keys_rot.reshape(local_rows, kv_width), values_local], axis=1)

    def visible_mask(block_start, sub_rows):
        key_seg = lax.dynamic_slice_in_dim(all_seg, block_start, sub_rows)
        key_index = block_start + jnp.arange(sub_rows, dtype=jnp.int32)
        visible = (local_seg[:, None] == key_seg[None, :]) & (
            query_index[:, None] >= key_index[None, :]
        )
        needed = (
            (block_start <= query_index[local_rows - 1])
            & (key_seg[0] <= local_seg[local_rows - 1])
            & (key_seg[sub_rows - 1] >= local_seg[0])
        )
        return (visible, needed)

    start_state = (
        jnp.full((KVH, group_size, local_rows), masked_value, jnp.float32),
        jnp.zeros((KVH, group_size, local_rows), jnp.float32),
        jnp.zeros((local_rows, KVH, group_size, HD), jnp.float32),
    )
    state = start_state
    piece = lax.all_gather(packed, "seq", axis=0, tiled=True)
    piece_rows = piece.shape[0]
    attend_sub_rows = block_size(piece_rows)
    kv_blocks = piece.reshape(piece_rows // attend_sub_rows, attend_sub_rows, 2 * kv_width)
    block_starts = attend_sub_rows * jnp.arange(piece_rows // attend_sub_rows, dtype=jnp.int32)

    def key_step(carried, pair_item):
        kv_block, block_start = pair_item
        visible, needed = visible_mask(block_start, attend_sub_rows)

        def update(running):
            running_max, running_sum, running_out = running
            key_block = kv_block[:, :kv_width].reshape(attend_sub_rows, KVH, HD)
            value_block = kv_block[:, kv_width:].reshape(attend_sub_rows, KVH, HD)
            scores = factor * jnp.einsum(
                "qkgd,jkd->kgqj", queries, key_block, preferred_element_type=jnp.float32
            )
            scores = jnp.where(visible, scores, masked_value)
            new_max = jnp.maximum(running_max, jnp.max(scores, axis=-1))
            weights = jnp.where(visible, jnp.exp(scores - new_max[..., None]), 0.0)
            rescale = jnp.exp(running_max - new_max)
            running_sum = running_sum * rescale + jnp.sum(weights, axis=-1)
            mixed = jnp.einsum(
                "kgqj,jkd->qkgd",
                weights.astype(jnp.bfloat16),
                value_block,
                preferred_element_type=jnp.float32,
            )
            running_out = running_out * jnp.transpose(rescale, (2, 0, 1))[..., None] + mixed
            return (new_max, running_sum, running_out)

        return (lax.cond(needed, update, lambda running: running, carried), None)

    state, unused = lax.scan(key_step, state, (kv_blocks, block_starts))
    running_max, running_sum, running_out = state
    attended_heads = running_out / jnp.transpose(running_sum, (2, 0, 1))[..., None]
    log_total = running_max + jnp.log(running_sum)
    attended_low = attended_heads.reshape(local_rows, H * HD).astype(jnp.bfloat16)
    middle = inputs + jnp.dot(attended_low, w_out, preferred_element_type=jnp.float32)
    inv_second = lax.rsqrt(jnp.mean(middle * middle, axis=-1, keepdims=True) + epsilon)
    scaled_second = middle * inv_second
    gain_second = gain_mlp.astype(jnp.float32)
    normed_mlp = (scaled_second * gain_second).astype(jnp.bfloat16)
    gate = jnp.dot(normed_mlp, w_gate, preferred_element_type=jnp.float32)
    up_proj = jnp.dot(normed_mlp, w_up, preferred_element_type=jnp.float32)
    sigmoid_gate = jax.nn.sigmoid(gate)
    silu_gate = gate * sigmoid_gate
    hidden = (silu_gate * up_proj).astype(jnp.bfloat16)
    result = middle + jnp.dot(hidden, w_down, preferred_element_type=jnp.float32)
    output = result.astype(jnp.bfloat16)[None]
    grad_down = contract_rows(hidden, cot_rows)
    d_hidden = times_transposed(cot_rows, w_down)
    d_gate = (d_hidden * up_proj * (sigmoid_gate + silu_gate * (1.0 - sigmoid_gate))).astype(
        jnp.bfloat16
    )
    d_up = (d_hidden * silu_gate).astype(jnp.bfloat16)
    grad_gate = contract_rows(normed_mlp, d_gate)
    grad_up = contract_rows(normed_mlp, d_up)
    d_normed_mlp = times_transposed(d_gate, w_gate) + times_transposed(d_up, w_up)
    grad_gain_mlp = jnp.sum(d_normed_mlp * scaled_second, axis=0)
    mixed_second = d_normed_mlp * gain_second
    d_middle = cot_rows.astype(jnp.float32) + inv_second * (
        mixed_second
        - scaled_second * jnp.mean(mixed_second * scaled_second, axis=-1, keepdims=True)
    )
    d_branch = d_middle.astype(jnp.bfloat16)
    grad_out = contract_rows(attended_low, d_branch)
    d_attended = times_transposed(d_branch, w_out).astype(jnp.bfloat16)
    d_heads = d_attended.reshape(local_rows, KVH, group_size, HD)
    delta = jnp.transpose(jnp.sum(d_heads.astype(jnp.float32) * attended_heads, axis=-1), (1, 2, 0))
    gathered = lax.all_gather(packed, "seq", axis=0, tiled=True)
    total_rows = gathered.shape[0]
    sub_rows = block_size(total_rows)
    kv_blocks = gathered.reshape(total_rows // sub_rows, sub_rows, 2 * kv_width)
    block_starts = sub_rows * jnp.arange(total_rows // sub_rows, dtype=jnp.int32)

    def back_step(d_queries, pair_item):
        kv_block, block_start = pair_item
        visible, needed = visible_mask(block_start, sub_rows)

        def compute(carried):
            key_block = kv_block[:, :kv_width].reshape(sub_rows, KVH, HD)
            value_block = kv_block[:, kv_width:].reshape(sub_rows, KVH, HD)
            scores = factor * jnp.einsum(
                "qkgd,jkd->kgqj", queries, key_block, preferred_element_type=jnp.float32
            )
            probs = jnp.where(visible, jnp.exp(scores - log_total[..., None]), 0.0)
            d_probs = jnp.einsum(
                "qkgd,jkd->kgqj", d_heads, value_block, preferred_element_type=jnp.float32
            )
            d_scores = (factor * probs * (d_probs - delta[..., None])).astype(jnp.bfloat16)
            carried = carried + jnp.einsum(
                "kgqj,jkd->qkgd", d_scores, key_block, preferred_element_type=jnp.float32
            )
            d_keys = jnp.einsum(
                "kgqj,qkgd->jkd", d_scores, queries, preferred_element_type=jnp.float32
            )
            d_values = jnp.einsum(
                "kgqj,qkgd->jkd",
                probs.astype(jnp.bfloat16),
                d_heads,
                preferred_element_type=jnp.float32,
            )
            return (
                carried,
                jnp.concatenate(
                    [d_keys.reshape(sub_rows, kv_width), d_values.reshape(sub_rows, kv_width)],
                    axis=1,
                ),
            )

        def skipped(carried):
            return (carried, jnp.zeros((sub_rows, 2 * kv_width), jnp.float32))

        return lax.cond(needed, compute, skipped, d_queries)

    d_queries, key_terms = lax.scan(
        back_step,
        jnp.zeros((local_rows, KVH, group_size, HD), jnp.float32),
        (kv_blocks, block_starts),
    )
    own_terms = lax.psum_scatter(
        key_terms.reshape(total_rows, 2 * kv_width).astype(jnp.bfloat16),
        "seq",
        scatter_dimension=0,
        tiled=True,
    ).astype(jnp.float32)
    own_keys = own_terms[:, :kv_width]
    own_values = own_terms[:, kv_width:]
    d_query_low = (
        rotate(d_queries.reshape(local_rows, H, HD), -local_pos)
        .reshape(local_rows, H * HD)
        .astype(jnp.bfloat16)
    )
    d_key_low = (
        rotate(own_keys.reshape(local_rows, KVH, HD), -local_pos)
        .reshape(local_rows, kv_width)
        .astype(jnp.bfloat16)
    )
    d_value_low = own_values.astype(jnp.bfloat16)
    grad_query = contract_rows(normed, d_query_low)
    grad_key = contract_rows(normed, d_key_low)
    grad_value = contract_rows(normed, d_value_low)
    d_normed = (
        times_transposed(d_query_low, w_query)
        + times_transposed(d_key_low, w_key)
        + times_transposed(d_value_low, w_value)
    )
    grad_gain_attn = jnp.sum(d_normed * scaled_first, axis=0)
    mixed_first = d_normed * gain_first
    d_inputs = d_middle + inv_first * (
        mixed_first - scaled_first * jnp.mean(mixed_first * scaled_first, axis=-1, keepdims=True)
    )
    summed = lax.psum(
        (
            grad_gain_attn,
            grad_query,
            grad_key,
            grad_value,
            grad_out,
            grad_gain_mlp,
            grad_gate,
            grad_up,
            grad_down,
        ),
        ("seq", "batch"),
    )
    (
        grad_gain_attn,
        grad_query,
        grad_key,
        grad_value,
        grad_out,
        grad_gain_mlp,
        grad_gate,
        grad_up,
        grad_down,
    ) = summed
    return (
        output,
        d_inputs[None],
        grad_gain_attn,
        grad_query,
        grad_key,
        grad_value,
        grad_out,
        grad_gain_mlp,
        grad_gate,
        grad_up,
        grad_down,
    )


def solution(mesh):
    placed = (
        P("batch", "seq", None),
        P("batch", "seq"),
        P(),
        P(),
        P(),
        P(),
        P(),
        P(),
        P(),
        P(),
        P(),
        P("batch", "seq", None),
    )
    return jax.shard_map(
        local,
        mesh=mesh,
        in_specs=placed,
        out_specs=(
            P("batch", "seq", None),
            P("batch", "seq", None),
            P(),
            P(),
            P(),
            P(),
            P(),
            P(),
            P(),
            P(),
            P(),
        ),
        check_vma=False,
    )
```

profile of v0, /device:TPU:0, one launch (start us, length us, event | category | flops | bytes accessed | tf_op | source)
XLA Modules:
  0.0 916.6 jit_solution(10634851856003936974)
XLA Ops:
  7.3 28.6 %all-gather = s32[1,4096]{1,0:T(1,128)} all-gather(s32[1,512]{1,0:T(1,128)} %param.21), channel_id=2, replica_groups=mesh['seq'=8,'batch'=4] {'seq'}, dimensions={1}, use_global_device_ids=true | all-gather | bytes 18432 | tf_op jit(solution)/shard_map/all_gather | solution.py:78
  37.8 2.3 convolution_convert_fusion.1
  49.8 1.8 fusion.52
  51.9 57.4 %all-gather.3.cloned.1.call-done = bf16[4096,384]{0,1:T(8,128)(2,1)} async-done(((bf16[512,384]{0,1:T(8,128)(2,1)}), bf16[4096,384]{0,1:T(8,128)(2,1)}) %all-gather.3.cloned.1.call-update) | async-done | bytes 3145744 | tf_op jit(solution)/shard_map/all_gather | solution.py:118
  109.3 4.0 copy.71
  115.0 73.5 %while.29 = (s32[]{:T(128)}, f32[3,3,512]{2,1,0:T(4,128)S(1)}, f32[3,3,512]{2,1,0:T(4,128)}, f32[512,3,3,64]{0,3,2,1:T(8,128)}, s32[4]{0:T(128)}, /*index=5*/s32...) while((s32[]{:T(128)}, f32[3,3,512]{2,1,0:T(4,128)S(1)}, ...), condition=%wide.region_8.9_spmd, body=%wide.region_3.8_spmd.sunk | while | flops 1271478784 | bytes 65929636 | solution.py:151
  124.6 34.9 %conditional.4 = ((f32[3,3,512]{2,1,0:T(4,128)S(1)}, f32[3,3,512]{2,1,0:T(4,128)}, f32[512,3,3,64]{0,3,2,1:T(8,128)})) conditional(s32[]{:T(128)} %convert_element_type.259, (f32[3,3,512]{2,1,0:T(4,128)S(1)}, f32[3,3,512]{2,1,0:T(4,128)}, f32[512,3,3,64]{0,3,2,1:T(8,128)}) %tuple.95, (s32[1,512]{1,0:T(1,128)S(1)}, s32[1024]{0:T(1024)S(1)}, ...), branch_computations={%region_4.4_spmd, %region_5.7_spmd} | conditional | flops 1271478784 | bytes 65916968 | solution.py:149
  128.8 8.0 fusion
  137.4 10.8 %fusion.2 = f32[3,3,512]{2,1,0:T(4,128)S(1)} fusion(f32[3,1024,512,3]{2,1,3,0:T(8,128)} %get-tuple-element.437, f32[3,3,512]{2,1,0:T(4,128)S(1)} %get-tuple-element.650, pred[512,1024]{0,1:T(8,128)(4,1)S(1)} %compare_and_fusion), kind=kLoop, calls=%fused_computation.4 | loop fusion | flops 23588352 | bytes 19435520 | tf_op jit(solution)/shard_map/while/body/eval_jaxpr/cond/branch_1_fun/reduce_sum | solution.py:139
  149.6 10.0 %fusion.9 = f32[512,3,3,64]{0,3,2,1:T(8,128)} fusion(bf16[1024,3,64,1]{0,2,3,1:T(8,128)(2,1)} %bitcast.242, f32[3,1024,512,3]{2,1,3,0:T(8,128)} %get-tuple-element.437, f32[3,3,512]{2,1,0:T(4,128)S(1)} %get-tuple-element.650, pred[512,1024]{0,1:T(8,128)(4,1)S(1)} %compare_and_fusion, f32[512,3,3,64]{0,3,2,1:T(8,128)} %get-tuple-element.234, ...), kind=kOutput, calls=%fused_computation.9 | convolution fusion | flops 628162560 | bytes 22188032 | tf_op jit(solution)/shard_map/while/body/eval_jaxpr/cond/branch_1_fun/kgqj,jkd->qkgd/dot_general | solution.py:140
  195.8 3.5 multiply_convert_fusion
  201.0 1.9 multiply_reduce_fusion
  209.3 97.5 %while.30 = (s32[]{:T(128)}, f32[512,3,3,64]{0,3,2,1:T(8,128)}, bf16[4,1024,384]{2,1,0:T(8,128)(2,1)}, s32[4]{0:T(128)}, s32[512]{0:T(512)}, /*index=5*/s32[4096...) while((s32[]{:T(128)}, f32[512,3,3,64]{0,3,2,1:T(8,128)}, ...), condition=%wide.region_15.16_spmd, body=%wide.region_12.15_spmd.sunk | while | flops 3075245056 | bytes 144399344 | solution.py:234
  218.9 46.1 %conditional.5 = (f32[512,3,3,64]{0,3,2,1:T(8,128)}, bf16[1,1024,384]{1,2,0:T(8,128)(2,1)S(1)}) conditional(s32[]{:T(128)} %convert_element_type.260, f32[512,3,3,64]{0,3,2,1:T(8,128)} %get-tuple-element.716, (s32[1,512]{1,0:T(1,128)S(1)}, s32[1024]{0:T(1024)S(1)}, s32[512]{0:T(512)}, s32[]{:T(128)}, s32[1,1024]{1,0:T(1,128)S(1)}, ...), branch_computations={%region_13.13_spmd, %region_14.14_spmd} | conditional | flops 3075245056 | bytes 138094672 | solution.py:232
  220.2 7.8 fusion.81
  230.2 10.2 %fusion.17 = bf16[3,3,512,1024]{2,3,1,0:T(8,128)(2,1)S(1)} fusion(f32[3,1024,512,3]{2,1,3,0:T(8,128)} %fusion.81, f32[3,3,512]{2,1,0:T(4,128)} %get-tuple-element.261, f32[3,3,512]{2,1,0:T(4,128)} %get-tuple-element.259, pred[512,1024]{0,1:T(8,128)(4,1)S(1)} %compare_and_fusion.1, bf16[1024,3,64,1]{0,2,3,1:T(8,128)(2,1)S(1)} %bitcast.243, ...), kind=kOutput, calls=%fused_computation.20 | convolution fusion | flops 637009920 | bytes 29855744 | tf_op jit(solution)/shard_map/while/body/eval_jaxpr/cond/branch_1_fun/qkgd,jkd->kgqj/dot_general | solution.py:205
  240.4 3.7 copy-done.1
  244.1 4.1 fusion.24
  248.1 10.2 %fusion.21 = bf16[3,1024,64,1]{1,2,3,0:T(8,128)(2,1)S(1)} fusion(bf16[512,3,3,64]{0,3,2,1:T(8,128)(2,1)} %get-tuple-element.260, f32[3,1024,512,3]{2,1,3,0:T(8,128)} %fusion.81, f32[3,3,512]{2,1,0:T(4,128)} %get-tuple-element.259, pred[512,1024]{0,1:T(8,128)(4,1)S(1)} %compare_and_fusion.1), kind=kOutput, calls=%fused_computation.25 | convolution fusion | flops 622854144 | bytes 20400128 | tf_op jit(solution)/shard_map/while/body/eval_jaxpr/cond/branch_1_fun/kgqj,qkgd->jkd/dot_general | solution.py:215
  258.4 6.6 fusion.82
  306.8 4.7 copy.49
  318.3 2.9 fusion.87
  321.2 2.9 fusion.88
  324.0 2.9 fusion.48
  326.9 300.4 %reduce-scatter.2.cloned.1.call-done = bf16[512,384]{0,1:T(8,128)(2,1)} async-done(((bf16[4096,384]{0,1:T(8,128)(2,1)}), bf16[512,384]{0,1:T(8,128)(2,1)}) %reduce-scatter.2.cloned.1.call-update) | async-done | bytes 393232 | tf_op jit(solution)/shard_map/reduce_scatter | solution.py:239
  632.5 3.7 fusion.37
  637.7 1.9 fusion.44
  639.5 41.5 %all-reduce = (f32[576]{0:T(1024)}, f32[576]{0:T(1024)}) all-reduce(f32[576]{0:T(1024)S(1)} %get-tuple-element.373, f32[576]{0:T(1024)} %get-tuple-element.371), channel_id=1, replica_groups=mesh['seq'=8,'batch'=4] {'seq','batch'}, use_global_device_ids=true, to_apply=%region_19.20 | all-reduce | flops 1152 | bytes 9216 | tf_op jit(solution)/shard_map/psum | solution.py:271
  681.0 2.6 fusion.43
  683.6 211.4 %all-reduce.4.cloned.1.call-done = (f32[576,576]{1,0:T(8,128)}, f32[576,192]{0,1:T(8,128)}, f32[576,192]{0,1:T(8,128)}, f32[576,576]{1,0:T(8,128)}, f32[576,1536...) async-done(((f32[576,576]{1,0:T(8,128)}, f32[576,192]{0,1:T(8,128)}, f32[576,192]{0,1:T(8,128)}, f32[576,576]{1,0:T(8,128)}, f32[576,1536]{1,0:T(8,128)}, ...) | async-done | bytes 14155792 | tf_op jit(solution)/shard_map/psum | solution.py:271
  895.1 2.7 copy.113
  904.6 1.8 copy.118
  (240 shorter events, 105.5 us)
Async XLA Ops:
  7.2 188.6 %copy-start = (bf16[1536,576]{0,1:T(8,128)(2,1)S(1)}, bf16[1536,576]{0,1:T(8,128)(2,1)}, u32[]{:S(2)}) copy-start(bf16[1536,576]{0,1:T(8,128)(2,1)} %param.30) | copy-start | bytes 5308420
  7.2 32.9 %copy-start.5 = (bf16[1,512,576]{1,2,0:T(8,128)(2,1)S(1)}, bf16[1,512,576]{1,2,0:T(8,128)(2,1)}, u32[]{:S(2)}) copy-start(bf16[1,512,576]{1,2,0:T(8,128)(2,1)} %param.20) | copy-start | bytes 1769476
  7.2 32.9 %copy-start.40 = (bf16[576,192]{0,1:T(8,128)(2,1)S(1)}, bf16[576,192]{0,1:T(8,128)(2,1)}, u32[]{:S(2)}) copy-start(bf16[576,192]{0,1:T(8,128)(2,1)} %param.24) | copy-start | bytes 663556
  7.2 102.1 %all-gather.3.cloned.1.call-start = ((), (), s32[]{:S(2)}) async-start(), calls=%async_computation.1 | async-start | bytes 3538944 | tf_op jit(solution)/shard_map/all_gather | solution.py:118
  36.5 13.3 %copy-start.43 = (f32[576]{0:T(1024)}, f32[576]{0:T(1024)S(1)}, u32[]{:S(2)}) copy-start(f32[576]{0:T(1024)S(1)} %convert_element_type.135) | copy-start | bytes 6916
  37.8 12.0 %copy-start.46 = (f32[512]{0:T(512)}, f32[512]{0:T(512)S(1)}, u32[]{:S(2)}) copy-start(f32[512]{0:T(512)S(1)} %add_rsqrt_fusion.1) | copy-start | bytes 6148
  41.2 5.8 copy-start.20
  45.2 3.0 copy-start.48
  47.0 580.3 %reduce-scatter.2.cloned.1.call-start = ((), (), s32[]{:S(2)}) async-start(), calls=%async_computation.2 | async-start | bytes 3538944 | tf_op jit(solution)/shard_map/reduce_scatter | solution.py:239
  109.3 5.8 copy-start.35
  190.8 13.5 %copy-start.8 = (f32[512,576]{0,1:T(8,128)}, f32[512,576]{0,1:T(8,128)S(1)}, u32[]{:S(2)}) copy-start(f32[512,576]{0,1:T(8,128)S(1)} %get-tuple-element.472) | copy-start | bytes 3538948
  204.7 3.5 copy-start.3
  205.3 4.0 copy-start.23
  220.2 10.0 %copy-start.24 = (bf16[512,3,3,64]{0,3,2,1:T(8,128)(2,1)S(1)}, bf16[512,3,3,64]{0,3,2,1:T(8,128)(2,1)}, u32[]{:S(2)}) copy-start(bf16[512,3,3,64]{0,3,2,1:T(8,128)(2,1)} %get-tuple-element.260) | copy-start | bytes 1769476 | tf_op jit(solution)/shard_map/while/body/eval_jaxpr/cond
  240.4 3.7 copy-start.1
  311.5 3.1 copy-start.6
  311.6 3.1 copy-start.44
  311.6 3.1 copy-start.47
  311.6 583.5 %all-reduce.4.cloned.1.call-start = ((), (), s32[]{:S(2)}) async-start(), calls=%async_computation.3 | async-start | bytes 29097984 | tf_op jit(solution)/shard_map/psum | solution.py:271
  318.3 2.9 copy-start.27
  321.2 2.9 copy-start.19
  321.2 2.9 copy-start.25
  628.2 3.0 copy-start.38
  632.4 3.8 copy-start.32
  632.4 3.8 copy-start.41
  632.5 4.2 copy-start.39
  895.0 2.7 copy-start.37
  895.0 3.5 copy-start.36
  895.1 4.3 copy-start.30
  898.6 2.7 copy-start.17
  901.3 3.3 copy-start.16
  904.6 3.3 copy-start.15
  (25 other events, 33.6 us)
Sparse Core Ops, SparseCore 0:
  47.1 62.1 all-gather.2
  311.7 315.5 reduce-scatter.1
  634.8 260.1 all-reduce.3
where the time goes:
time: 929 us; the launch traced here: 917 us
  waiting for transfers between devices  569 us (61%)
  matrix products  93.9 us (10%)
  local copies, waits for them, and re-layouts  85.4 us (9%)
  blocking collectives  70.1 us (8%)
  loops' own time  46.6 us (5%)
  other arithmetic  36.3 us (4%)
  between operations  14.7 us (2%)
    reduce_scatter x1, waiting for transfers between devices, local(): lax.psum_scatter(key_terms.reshape(total_rows, 2 * kv_width).astype(jnp.b...  300 us
    psum x1, waiting for transfers between devices, local(): lax.psum((grad_gain_attn, grad_query, grad_key, grad_value, grad_out, gra...  211 us
    all_gather x1, waiting for transfers between devices, local(): piece = lax.all_gather(packed, 'seq', axis=0, tiled=True)  57.4 us
    psum x1, blocking collectives, local(): lax.psum((grad_gain_attn, grad_query, grad_key, grad_value, grad_out, gra...  41.5 us
    all_gather x1, blocking collectives, local(): all_seg = lax.all_gather(local_seg, 'seq', axis=0, tiled=True)  28.6 us
    another operation x1, loops' own time, local(): state, unused = lax.scan(key_step, state, (kv_blocks, block_starts))  23.5 us
    another operation x1, loops' own time, local(): lax.scan(back_step, jnp.zeros((local_rows, KVH, group_size, HD), jnp.floa...  22.8 us
    unnamed x104, local copies, waits for them, and re-layouts  22.3 us
  transfers between devices with their start and end apart: 3, of which 3 were waited for; matrix products, arithmetic and copies ran while one was open for 3% of the time, Pallas kernels for 0%

commit v1 on v0

v1 whole, which is shorter than its diff:
```python
import functools

import jax
import jax.numpy as jnp
import numpy as np
from jax import lax
from jax.experimental import pallas as pl
from jax.experimental.pallas import tpu as pltpu
from jax.sharding import PartitionSpec as P

H = 9
KVH = 3
HD = 64
GROUP = H // KVH
PAIR = 2 * HD
META = 16

epsilon = 1e-05
theta_base = 10000.0
masked_value = -1e30
never = 1e30
LOG2E = 1.4426950408889634
LN2 = 0.6931471805599453
MESH = pl.DeviceIdType.MESH
f32 = jnp.float32
bf16 = jnp.bfloat16
VMEM_LIMIT = 60 * 2**20


def dot(left, right, left_dim, right_dim):
    return lax.dot_general(
        left,
        right,
        (((left_dim,), (right_dim,)), ((), ())),
        preferred_element_type=f32,
    )


def angle_table(ranks, rows):
    half = HD // 2
    freqs = theta_base ** (-2.0 * np.arange(half, dtype=np.float64) / HD)
    angles = freqs[:, None] * np.arange(ranks * rows, dtype=np.float64)[None, :]
    table = np.concatenate([np.cos(angles), np.sin(angles)], axis=0).astype(np.float32)
    return np.ascontiguousarray(table.reshape(HD, ranks, rows).transpose(1, 0, 2))


def turn(vectors, cosine, sine):
    half = HD // 2
    first, second = vectors[:half], vectors[half:]
    return jnp.concatenate(
        [first * cosine - second * sine, second * cosine + first * sine], axis=0
    )


def turn_back(vectors, cosine, sine):
    half = HD // 2
    first, second = vectors[:half], vectors[half:]
    return jnp.concatenate(
        [first * cosine + second * sine, second * cosine - first * sine], axis=0
    )


def own_bias(seg_row):
    rows = seg_row.shape[1]
    ids = seg_row.astype(f32)
    columns = jnp.broadcast_to(ids, (128, rows)).T[:, :1]
    key = lax.broadcasted_iota(jnp.int32, (rows, rows), 0)
    query = lax.broadcasted_iota(jnp.int32, (rows, rows), 1)
    visible = (columns == ids) & (key <= query)
    return jnp.where(visible, 0.0, masked_value)


def long_row(seg_row):
    return seg_row == seg_row[:, :1]


def first_bias(meta, rows):
    start = 2.0 * meta[0:1, :1].astype(f32) + meta[1:2, :1].astype(f32)
    key = lax.broadcasted_iota(jnp.int32, (rows, 1), 0).astype(f32)
    return jnp.where(key >= start, 0.0, masked_value)


def attend_kernel(
    ranks,
    tokens_ref,
    seg_ref,
    gain_ref,
    wq_ref,
    wk_ref,
    wv_ref,
    table_ref,
    qt_ref,
    kv_ref,
    att_ref,
    lse_ref,
    turn_ref,
    max_ref,
    sum_ref,
    turn_sem,
    z_sem,
    x_sem,
    in_sem,
):
    rank = lax.axis_index("seq")
    row = lax.axis_index("batch")
    rows = tokens_ref.shape[0]
    depth = lax.div(rank, 2)
    odd = lax.rem(rank, 2)
    mate = rank + 1 - 2 * odd
    has_up = rank + 2 < ranks
    has_down = rank >= 2

    turn_copy = pltpu.make_async_copy(table_ref.at[rank], turn_ref, turn_sem)
    turn_copy.start()

    barrier = pltpu.get_barrier_semaphore()
    pl.semaphore_signal(barrier, inc=1, device_id=(mate, row), device_id_type=MESH)

    @pl.when(has_up)
    def _():
        pl.semaphore_signal(barrier, inc=1, device_id=(rank + 2, row), device_id_type=MESH)

    @pl.when(has_down)
    def _():
        pl.semaphore_signal(barrier, inc=1, device_id=(rank - 2, row), device_id_type=MESH)

    def z_copy(block, group):
        return pltpu.make_async_remote_copy(
            src_ref=kv_ref.at[block, group],
            dst_ref=kv_ref.at[block, group],
            send_sem=z_sem.at[block, group],
            recv_sem=in_sem.at[block, group],
            device_id=(rank + 2, row),
            device_id_type=MESH,
        )

    def x_copy(block, group):
        return pltpu.make_async_remote_copy(
            src_ref=kv_ref.at[block, group],
            dst_ref=kv_ref.at[block, group],
            send_sem=x_sem.at[block, group],
            recv_sem=in_sem.at[block, group],
            device_id=(mate, row),
            device_id_type=MESH,
        )

    inputs = tokens_ref[...].astype(f32)
    inverse = lax.rsqrt(jnp.mean(inputs * inputs, axis=-1, keepdims=True) + epsilon)
    normed = (inputs * inverse * gain_ref[...].astype(f32)).astype(bf16)
    keys = dot(wk_ref[...], normed, 0, 1)
    values = dot(wv_ref[...], normed, 0, 1)
    seg_row = seg_ref[...]
    start = jnp.sum((seg_row != seg_row[:, rows - 1 :]).astype(f32), axis=1, keepdims=True)
    high = jnp.floor(0.5 * start)
    low = start - 2.0 * high
    which = lax.broadcasted_iota(jnp.int32, (META, PAIR), 0)
    meta = jnp.where(which == 0, high, jnp.where(which == 1, low, 0.0)).astype(bf16)
    turn_copy.wait()
    cosine = turn_ref[: HD // 2]
    sine = turn_ref[HD // 2 :]
    for group in range(KVH):
        part = slice(group * HD, group * HD + HD)
        both = jnp.concatenate([turn(keys[part], cosine, sine), values[part]], axis=0)
        kv_ref[rank, group, :rows, :] = both.astype(bf16).T
        kv_ref[rank, group, rows:, :] = meta

    pl.semaphore_wait(barrier, 1 + has_up.astype(jnp.int32) + has_down.astype(jnp.int32))
    for group in range(KVH):

        @pl.when(odd == 0)
        def _():
            x_copy(rank, group).start()

        @pl.when(has_up)
        def _():
            z_copy(rank, group).start()

    def relay(level, group):
        block = rank - 2 * level
        z_in = pltpu.make_async_remote_copy(
            src_ref=kv_ref.at[block, group],
            dst_ref=kv_ref.at[block, group],
            send_sem=z_sem.at[block, group],
            recv_sem=in_sem.at[block, group],
            device_id=(mate, row),
            device_id_type=MESH,
        )
        z_in.wait_recv()
        x_copy(block, group).start()

        @pl.when(has_up)
        def _():
            z_copy(block, group).start()

    queries = dot(wq_ref[...], normed, 0, 1)
    for head in range(H):
        part = slice(head * HD, head * HD + HD)
        turned = turn(queries[part], cosine, sine) * (LOG2E / HD**0.5)
        qt_ref[head, :HD, :] = turned.astype(bf16)
        qt_ref[head, HD:, :] = jnp.zeros((HD, rows), bf16)

    bias = own_bias(seg_row)
    for group in range(KVH):
        pair = kv_ref[rank, group, :rows, :]
        values_t = pair.T[HD:]
        for head in range(group * GROUP, (group + 1) * GROUP):
            scores = dot(pair, qt_ref[head], 1, 0) + bias
            top = jnp.max(scores, axis=0, keepdims=True)
            weights = jnp.exp2(scores - top)
            max_ref[head : head + 1, :] = top
            sum_ref[head : head + 1, :] = jnp.sum(weights, axis=0, keepdims=True)
            att_ref[head * HD : (head + 1) * HD, :] = dot(values_t, weights.astype(bf16), 1, 0)

        @pl.when(depth >= 1)
        def _():
            relay(1, group)

    in_long = long_row(seg_row)

    def block_step(block, group, key_bias):
        pair = kv_ref[block, group, :rows, :]
        values_t = pair.T[HD:]
        heads = range(group * GROUP, (group + 1) * GROUP)
        old_max = [max_ref[head : head + 1, :] for head in heads]
        old_sum = [sum_ref[head : head + 1, :] for head in heads]
        old_att = [att_ref[head * HD : (head + 1) * HD, :] for head in heads]
        results = []
        for spot, head in enumerate(heads):
            scores = dot(pair, qt_ref[head], 1, 0)
            if key_bias is not None:
                scores = scores + key_bias
            top = jnp.maximum(old_max[spot], jnp.max(scores, axis=0, keepdims=True))
            top = jnp.where(in_long, top, old_max[spot])
            weights = jnp.exp2(scores - jnp.where(in_long, top, never))
            scale = jnp.exp2(old_max[spot] - top)
            results.append(
                (
                    top,
                    old_sum[spot] * scale + jnp.sum(weights, axis=0, keepdims=True),
                    old_att[spot] * scale + dot(values_t, weights.astype(bf16), 1, 0),
                )
            )
        for spot, head in enumerate(heads):
            max_ref[head : head + 1, :] = results[spot][0]
            sum_ref[head : head + 1, :] = results[spot][1]
            att_ref[head * HD : (head + 1) * HD, :] = results[spot][2]

    def step(index, carry):
        level = lax.div(index + 1, 2)
        straight = lax.rem(index, 2) == 1
        block = jnp.where(straight, rank, mate) - 2 * level
        for group in range(KVH):

            @pl.when(straight & (level + 1 <= depth))
            def _():
                relay(level + 1, group)

            @pl.when(jnp.logical_not(straight))
            def _():
                x_copy(block, group).wait_recv()

            @pl.when(block == 0)
            def _():
                key_bias = first_bias(kv_ref[0, group, rows:, :], rows)
                block_step(block, group, key_bias)

            @pl.when(block != 0)
            def _():
                block_step(block, group, None)

        return carry

    lax.fori_loop(1 - odd, 2 * depth + 1, step, 0)

    for head in range(H):
        part = slice(head * HD, (head + 1) * HD)
        total = sum_ref[head : head + 1, :]
        att_ref[part, :] = att_ref[part, :] / total
        lse_ref[head : head + 1, :] = max_ref[head : head + 1, :] + jnp.log2(total)
    lse_ref[H:, :] = jnp.zeros_like(lse_ref[H:, :])

    def sent(level, carry):
        block = rank - 2 * level
        for group in range(KVH):

            @pl.when(has_up)
            def _():
                z_copy(block, group).wait_send()

            @pl.when((odd == 0) | (level >= 1))
            def _():
                x_copy(block, group).wait_send()

        return carry

    lax.fori_loop(0, depth + 1, sent, 0)


def attend(tokens, seg_row, gain, wq, wk, wv, ranks):
    rows, width = tokens.shape
    vmem = pl.BlockSpec(memory_space=pltpu.VMEM)
    table = jnp.asarray(angle_table(ranks, rows))
    dma = pltpu.SemaphoreType.DMA
    return pl.pallas_call(
        functools.partial(attend_kernel, ranks),
        out_shape=(
            jax.ShapeDtypeStruct((H, PAIR, rows), bf16),
            jax.ShapeDtypeStruct((ranks, KVH, rows + META, PAIR), bf16),
            jax.ShapeDtypeStruct((H * HD, rows), f32),
            jax.ShapeDtypeStruct((16, rows), f32),
        ),
        in_specs=[vmem] * 6 + [pl.BlockSpec(memory_space=pl.ANY)],
        out_specs=(vmem,) * 4,
        scratch_shapes=[
            pltpu.VMEM((HD, rows), f32),
            pltpu.VMEM((16, rows), f32),
            pltpu.VMEM((16, rows), f32),
            dma(()),
            dma((ranks, KVH)),
            dma((ranks, KVH)),
            dma((ranks, KVH)),
        ],
        compiler_params=pltpu.CompilerParams(
            collective_id=0, has_side_effects=True, vmem_limit_bytes=VMEM_LIMIT
        ),
        name="attend",
    )(tokens, seg_row, gain, wq, wk, wv, table)


def mlp_kernel(
    tokens_ref,
    cot_ref,
    att_ref,
    w_out_ref,
    gain_ref,
    w_gate_ref,
    w_up_ref,
    w_down_ref,
    out_ref,
    grads_ref,
    grad_out_ref,
    gain_grad_ref,
    d_middle_ref,
    dot_ref,
    delta_ref,
):
    rows, width = tokens_ref.shape
    hidden_units = w_gate_ref.shape[1]
    chunk = 512
    inputs = tokens_ref[...].astype(f32)
    attended = att_ref[...].astype(bf16).T
    middle = inputs + dot(attended, w_out_ref[...], 1, 0)
    inverse = lax.rsqrt(jnp.mean(middle * middle, axis=-1, keepdims=True) + epsilon)
    scaled = middle * inverse
    gain = gain_ref[...].astype(f32)
    normed = (scaled * gain).astype(bf16)
    normed_t = normed.T
    cot = cot_ref[...]
    cot_t = cot.T
    result = middle
    d_normed = jnp.zeros((rows, width), f32)
    for first in range(0, hidden_units, chunk):
        part = slice(first, first + chunk)
        gate = dot(normed, w_gate_ref[:, part], 1, 0)
        up = dot(normed, w_up_ref[:, part], 1, 0)
        d_hidden = dot(cot, w_down_ref[part, :], 1, 1)
        sigmoid = jax.nn.sigmoid(gate)
        silu = gate * sigmoid
        hidden = (silu * up).astype(bf16)
        d_gate = (d_hidden * up * (sigmoid + silu * (1.0 - sigmoid))).astype(bf16)
        d_up = (d_hidden * silu).astype(bf16)
        result = result + dot(hidden, w_down_ref[part, :], 1, 0)
        d_normed = d_normed + dot(d_gate, w_gate_ref[:, part], 1, 1)
        d_normed = d_normed + dot(d_up, w_up_ref[:, part], 1, 1)
        grads_ref[0, :, part] = dot(normed_t, d_gate, 1, 0).astype(bf16)
        grads_ref[1, :, part] = dot(normed_t, d_up, 1, 0).astype(bf16)
        grads_ref[2, :, part] = dot(cot_t, hidden, 1, 0).astype(bf16)
    out_ref[...] = result.astype(bf16)
    gain_grad_ref[...] = jnp.sum(d_normed * scaled, axis=0, keepdims=True)
    mixed = d_normed * gain
    d_middle = cot.astype(f32) + inverse * (
        mixed - scaled * jnp.mean(mixed * scaled, axis=-1, keepdims=True)
    )
    d_middle_ref[...] = d_middle
    d_branch = d_middle.astype(bf16)
    grad_out_ref[...] = dot(att_ref[...].astype(bf16), d_branch, 1, 0).astype(bf16)
    d_attended = dot(w_out_ref[...], d_branch, 1, 1).astype(bf16)
    for head in range(H):
        part = slice(head * HD, (head + 1) * HD)
        dot_ref[head, :HD, :] = jnp.zeros((HD, rows), bf16)
        dot_ref[head, HD:, :] = d_attended[part]
        delta_ref[head : head + 1, :] = jnp.sum(
            d_attended[part].astype(f32) * att_ref[part, :], axis=0, keepdims=True
        )
    delta_ref[H:, :] = jnp.zeros_like(delta_ref[H:, :])


def mlp(tokens, cot, att, w_out, gain, w_gate, w_up, w_down):
    rows, width = tokens.shape
    hidden_units = w_gate.shape[1]
    vmem = pl.BlockSpec(memory_space=pltpu.VMEM)
    return pl.pallas_call(
        mlp_kernel,
        out_shape=(
            jax.ShapeDtypeStruct((rows, width), bf16),
            jax.ShapeDtypeStruct((3, width, hidden_units), bf16),
            jax.ShapeDtypeStruct((H * HD, width), bf16),
            jax.ShapeDtypeStruct((1, width), f32),
            jax.ShapeDtypeStruct((rows, width), f32),
            jax.ShapeDtypeStruct((H, PAIR, rows), bf16),
            jax.ShapeDtypeStruct((16, rows), f32),
        ),
        in_specs=[vmem] * 8,
        out_specs=(vmem,) * 7,
        compiler_params=pltpu.CompilerParams(vmem_limit_bytes=VMEM_LIMIT),
        name="mlp",
    )(tokens, cot, att, w_out, gain, w_gate, w_up, w_down)


def back_kernel(
    ranks,
    seg_ref,
    turn_ref,
    qt_ref,
    kv_ref,
    lse_ref,
    dot_ref,
    delta_ref,
    terms_ref,
    dq_ref,
    acc_ref,
):
    rank = lax.axis_index("seq")
    rows = seg_ref.shape[1]
    seg_row = seg_ref[...]
    in_long = long_row(seg_row)
    acc_ref[...] = jnp.zeros_like(acc_ref)

    def pair_step(block, group, bias, level_of):
        pair = kv_ref[block, group, :rows, :]
        keys_t = pair.T[:HD]
        heads = range(group * GROUP, (group + 1) * GROUP)
        old = [acc_ref[head] for head in heads]
        total = jnp.zeros((rows, PAIR), f32)
        results = []
        for spot, head in enumerate(heads):
            scores = dot(pair, qt_ref[head], 1, 0)
            if bias is not None:
                scores = scores + bias
            probs = jnp.exp2(scores - level_of(lse_ref[head : head + 1, :]))
            d_probs = dot(pair, dot_ref[head], 1, 0)
            d_scores = (probs * (d_probs - delta_ref[head : head + 1, :])).astype(bf16)
            total = total + dot(probs.astype(bf16), dot_ref[head], 1, 1)
            total = total + dot(d_scores, qt_ref[head], 1, 1)
            results.append(old[spot] + dot(keys_t, d_scores, 1, 0))
        for spot, head in enumerate(heads):
            acc_ref[head] = results[spot]
        terms_ref[block, group] = total.astype(bf16)

    def level_off(lse):
        return jnp.where(in_long, lse, never)

    def step(block, carry):
        @pl.when(block == 0)
        def _():
            for group in range(KVH):
                key_bias = first_bias(kv_ref[0, group, rows:, :], rows)
                pair_step(block, group, key_bias, level_off)

        @pl.when(block != 0)
        def _():
            for group in range(KVH):
                pair_step(block, group, None, level_off)

        return carry

    lax.fori_loop(0, rank, step, 0)
    bias = own_bias(seg_row)
    for group in range(KVH):
        pair_step(rank, group, bias, lambda lse: lse)

    def clear(block, carry):
        terms_ref[block] = jnp.zeros((KVH, rows, PAIR), bf16)
        return carry

    lax.fori_loop(rank + 1, ranks, clear, 0)
    cosine = turn_ref[: HD // 2]
    sine = turn_ref[HD // 2 :]
    for head in range(H):
        part = slice(head * HD, (head + 1) * HD)
        dq_ref[part, :] = turn_back(acc_ref[head] * HD**-0.5, cosine, sine).astype(bf16)


def back(seg_row, turn_table, qt, kv, lse, dot_t, delta, ranks):
    rows = seg_row.shape[1]
    vmem = pl.BlockSpec(memory_space=pltpu.VMEM)
    return pl.pallas_call(
        functools.partial(back_kernel, ranks),
        out_shape=(
            jax.ShapeDtypeStruct((ranks, KVH, rows, PAIR), bf16),
            jax.ShapeDtypeStruct((H * HD, rows), bf16),
        ),
        in_specs=[vmem] * 7,
        out_specs=(vmem,) * 2,
        scratch_shapes=[pltpu.VMEM((H, HD, rows), f32)],
        compiler_params=pltpu.CompilerParams(vmem_limit_bytes=VMEM_LIMIT),
        name="back",
    )(seg_row, turn_table, qt, kv, lse, dot_t, delta)


def last_kernel(
    tokens_ref,
    gain_ref,
    wq_ref,
    wk_ref,
    wv_ref,
    turn_ref,
    dq_ref,
    own_ref,
    d_middle_ref,
    out_ref,
    grads_ref,
    gain_grad_ref,
    dk_ref,
    dv_ref,
):
    cosine = turn_ref[: HD // 2]
    sine = turn_ref[HD // 2 :]
    for group in range(KVH):
        part = slice(group * HD, (group + 1) * HD)
        both = own_ref[group].astype(f32).T
        dk_ref[part, :] = turn_back(both[:HD] * LN2, cosine, sine).astype(bf16)
        dv_ref[part, :] = both[HD:].astype(bf16)
    inputs = tokens_ref[...].astype(f32)
    inverse = lax.rsqrt(jnp.mean(inputs * inputs, axis=-1, keepdims=True) + epsilon)
    scaled = inputs * inverse
    gain = gain_ref[...].astype(f32)
    normed_t = (scaled * gain).astype(bf16).T
    q_cols = H * HD
    k_cols = KVH * HD
    grads_ref[:, :q_cols] = dot(normed_t, dq_ref[...], 1, 1).astype(bf16)
    grads_ref[:, q_cols : q_cols + k_cols] = dot(normed_t, dk_ref[...], 1, 1).astype(bf16)
    grads_ref[:, q_cols + k_cols :] = dot(normed_t, dv_ref[...], 1, 1).astype(bf16)
    d_normed = (
        dot(dq_ref[...], wq_ref[...], 0, 1)
        + dot(dk_ref[...], wk_ref[...], 0, 1)
        + dot(dv_ref[...], wv_ref[...], 0, 1)
    )
    gain_grad_ref[...] = jnp.sum(d_normed * scaled, axis=0, keepdims=True)
    mixed = d_normed * gain
    out_ref[...] = d_middle_ref[...] + inverse * (
        mixed - scaled * jnp.mean(mixed * scaled, axis=-1, keepdims=True)
    )


def last(tokens, gain, wq, wk, wv, turn_table, dq, own, d_middle):
    rows, width = tokens.shape
    vmem = pl.BlockSpec(memory_space=pltpu.VMEM)
    return pl.pallas_call(
        last_kernel,
        out_shape=(
            jax.ShapeDtypeStruct((rows, width), f32),
            jax.ShapeDtypeStruct((width, (H + 2 * KVH) * HD), bf16),
            jax.ShapeDtypeStruct((1, width), f32),
        ),
        in_specs=[vmem] * 9,
        out_specs=(vmem,) * 3,
        scratch_shapes=[
            pltpu.VMEM((KVH * HD, rows), bf16),
            pltpu.VMEM((KVH * HD, rows), bf16),
        ],
        compiler_params=pltpu.CompilerParams(vmem_limit_bytes=VMEM_LIMIT),
        name="last",
    )(tokens, gain, wq, wk, wv, turn_table, dq, own, d_middle)


def local(
    ranks,
    tokens,
    segment_ids,
    gain_attn,
    w_query,
    w_key,
    w_value,
    w_out,
    gain_mlp,
    w_gate,
    w_up,
    w_down,
    cotangent,
):
    rows, width = tokens.shape[1:]
    rank = lax.axis_index("seq")
    both_axes = ("seq", "batch")
    gain_first = gain_attn.reshape(1, width)
    gain_second = gain_mlp.reshape(1, width)
    qt, kv, att, lse = attend(
        tokens[0], segment_ids, gain_first, w_query, w_key, w_value, ranks
    )
    output, grads, grad_out, grad_gain_mlp, d_middle, dot_t, delta = mlp(
        tokens[0], cotangent[0], att, w_out, gain_second, w_gate, w_up, w_down
    )
    grads, grad_out = lax.psum((grads, grad_out), both_axes)
    turn_table = lax.dynamic_index_in_dim(
        jnp.asarray(angle_table(ranks, rows)), rank, keepdims=False
    )
    terms, dq = back(segment_ids, turn_table, qt, kv, lse, dot_t, delta, ranks)
    own = lax.psum_scatter(terms, "seq", scatter_dimension=0, tiled=True)[0]
    d_inputs, late, grad_gain_attn = last(
        tokens[0], gain_first, w_query, w_key, w_value, turn_table, dq, own, d_middle
    )
    late = lax.psum(late, both_axes)
    grad_gain_attn, grad_gain_mlp = lax.psum((grad_gain_attn, grad_gain_mlp), both_axes)
    q_cols = H * HD
    k_cols = KVH * HD
    return (
        output[None],
        d_inputs[None],
        grad_gain_attn[0],
        late[:, :q_cols].astype(f32),
        late[:, q_cols : q_cols + k_cols].astype(f32),
        late[:, q_cols + k_cols :].astype(f32),
        grad_out.astype(f32),
        grad_gain_mlp[0],
        grads[0].astype(f32),
        grads[1].astype(f32),
        grads[2].T.astype(f32),
    )


def solution(mesh):
    split = P("batch", "seq", None)
    return jax.shard_map(
        functools.partial(local, mesh.shape["seq"]),
        mesh=mesh,
        in_specs=(split, P("batch", "seq")) + (P(),) * 9 + (split,),
        out_specs=(split, split) + (P(),) * 9,
        check_vma=False,
    )
```

time: 929 us -> 421 us (0.45)
  waiting for transfers between devices: 569 us -> 266 us
  matrix products: 93.9 us -> 0 us
  local copies, waits for them, and re-layouts: 85.4 us -> 16.7 us
  Pallas kernels: 0 us -> 66.3 us
  loops' own time: 46.6 us -> 0 us
  blocking collectives: 70.1 us -> 41.2 us
  other arithmetic: 36.3 us -> 11 us
    reduce_scatter x1, waiting for transfers between devices: 300 us -> 143 us  [local(): own = lax.psum_scatter(terms, 'seq', scatter_dimension=0, tiled=True)[0]]
    dot_general x28 -> x0, matrix products: 93.9 us -> none  [the longest x7 14.7 us: contract_rows(): lax.dot_general(left, right, (((0,), (0,)), ((), ())), preferred_element_...]
    psum x1, waiting for transfers between devices: 211 us -> 123 us  [local(): late = lax.psum(late, both_axes)]
    pallas_call x0 -> x4, Pallas kernels: none -> 66.3 us  [the longest x1 21 us: attend(): pl.pallas_call(functools.partial(attend_kernel, ranks), out_shape=(jax.Sh...]
    all_gather x1 -> x0, waiting for transfers between devices: 57.4 us -> none  [local(): piece = lax.all_gather(packed, 'seq', axis=0, tiled=True)]
    another operation x10 -> x0, loops' own time: 46.6 us -> none  [the longest x1 23.5 us: local(): state, unused = lax.scan(key_step, state, (kv_blocks, block_starts))]
    all_gather x1 -> x0, blocking collectives: 28.6 us -> none  [local(): all_seg = lax.all_gather(local_seg, 'seq', axis=0, tiled=True)]
    slice x20 -> x0, local copies, waits for them, and re-layouts: 16.4 us -> none  [the longest x8 9.55 us: visible_mask(): query_index[local_rows - 1]]
  transfers between devices with their start and end apart: 3 -> 2, of which waited for: 3 -> 2; matrix products, arithmetic and copies ran while one was open for 3% -> 1% of each run, Pallas kernels for 0% -> 0%
where the time goes in v1:
time: 421 us; the launch traced here: 416 us
  waiting for transfers between devices  266 us (63%)
  Pallas kernels  66.3 us (16%)
  blocking collectives  41.2 us (10%)
  local copies, waits for them, and re-layouts  16.7 us (4%)
  between operations  14.3 us (3%)
  other arithmetic  11 us (3%)
    reduce_scatter x1, waiting for transfers between devices, local(): own = lax.psum_scatter(terms, 'seq', scatter_dimension=0, tiled=True)[0]  143 us
    psum x1, waiting for transfers between devices, local(): late = lax.psum(late, both_axes)  123 us
    psum x1, blocking collectives, local(): lax.psum((grad_gain_attn, grad_gain_mlp), both_axes)  41.2 us
    pallas_call x1, Pallas kernels, attend(): pl.pallas_call(functools.partial(attend_kernel, ranks), out_shape=(jax.Sh...  21 us
    pallas_call x1, Pallas kernels, back(): pl.pallas_call(functools.partial(back_kernel, ranks), out_shape=(jax.Shap...  20 us
    pallas_call x1, Pallas kernels, mlp(): pl.pallas_call(mlp_kernel, out_shape=(jax.ShapeDtypeStruct((rows, width),...  18.9 us
    unnamed x31, local copies, waits for them, and re-layouts  13.9 us
  transfers between devices with their start and end apart: 2, of which 2 were waited for; matrix products, arithmetic and copies ran while one was open for 1% of the time, Pallas kernels for 0%

profile of v1, /device:TPU:0, one launch (start us, length us, event | category | flops | bytes accessed | tf_op | source)
XLA Modules:
  0.0 415.8 jit_solution(13801525023328192280)
XLA Ops:
  7.2 0.0 reduce-scatter.2.cloned.1.call-start
  7.3 2.3 copy.25
  9.5 1.8 copy.27.wk_ref
  11.4 0.9 copy.28.wv_ref
  12.2 0.6 reshape.34.gain_ref
  12.8 2.3 copy.29.w_down_ref
  15.1 1.1 copy.26
  16.2 0.6 reshape.35.gain_ref
  16.7 1.6 dynamic-slice_bitcast_fusion.turn_ref
  18.3 21.0 %attend.1 = (bf16[9,128,512]{2,1,0:T(8,128)(2,1)}, bf16[8,3,528,128]{3,2,1,0:T(8,128)(2,1)}, f32[576,512]{1,0:T(8,128)}, f32[16,512]{1,0:T(8,128)}) custom-call(bf16[512,576]{1,0:T(8,128)(2,1)} %bitcast.24, s32[1,512]{1,0:T(1,128)} %seg_ref.3, bf16[1,576]{1,0:T(2,128)(2,1)} %reshape.34.gain_ref, bf16[576,576]{1,0:T(8,128)(2,1)} %wq_ref.3, ...), custom_call_target="tpu_custom_call" | custom-call | tf_op jit(solution)/shard_map/attend/pallas_call | solution.py:304
  39.3 18.9 %mlp.1 = (bf16[512,576]{1,0:T(8,128)(2,1)}, bf16[3,576,1536]{2,1,0:T(8,128)(2,1)}, bf16[576,576]{1,0:T(8,128)(2,1)}, f32[1,576]{1,0:T(1,128)}, f32[512,576]{1,0:...) custom-call(bf16[512,576]{1,0:T(8,128)(2,1)} %bitcast.25, bf16[512,576]{1,0:T(8,128)(2,1)} %bitcast.27, ...), custom_call_target="tpu_custom_call" | custom-call | tf_op jit(solution)/shard_map/mlp/pallas_call | solution.py:402
  58.2 20.0 %back.1 = (bf16[8,3,512,128]{3,2,1,0:T(8,128)(2,1)}, bf16[576,512]{1,0:T(8,128)(2,1)}) custom-call(s32[1,512]{1,0:T(1,128)} %seg_ref.3, f32[64,512]{1,0:T(8,128)} %dynamic-slice_bitcast_fusion.turn_ref, bf16[9,128,512]{2,1,0:T(8,128)(2,1)} %get-tuple-element.29.qt_ref, bf16[8,3,528,128]{3,2,1,0:T(8,128)(2,1)} %get-tuple-element.30.kv_ref, ...), custom_call_target="tpu_custom_call" | custom-call | tf_op jit(solution)/shard_map/back/pallas_call | solution.py:497
  78.2 0.0 reduce-scatter.2.cloned.1.call-update
  78.3 0.0 all-reduce.4.cloned.1.call-start
  78.3 143.4 %reduce-scatter.2.cloned.1.call-done = bf16[1,3,512,128]{3,2,1,0:T(8,128)(2,1)} async-done(((bf16[8,3,512,128]{3,2,1,0:T(8,128)(2,1)}), bf16[1,3,512,128]{3,2,1,0:T(8,128)(2,1)}) %reduce-scatter.2.cloned.1.call-update) | async-done | bytes 393232 | tf_op jit(solution)/shard_map/reduce_scatter | solution.py:608
  221.7 6.4 %last.1 = (f32[512,576]{1,0:T(8,128)}, bf16[576,960]{1,0:T(8,128)(2,1)}, f32[1,576]{1,0:T(1,128)}) custom-call(bf16[512,576]{1,0:T(8,128)(2,1)} %bitcast.26, bf16[1,576]{1,0:T(2,128)(2,1)} %reshape.34.gain_ref, bf16[576,576]{1,0:T(8,128)(2,1)} %wq_ref.3, bf16[576,192]{1,0:T(8,128)(2,1)} %copy.27.wk_ref, bf16[576,192]{1,0:T(8,128)(2,1)} %copy.28.wv_ref, ...), custom_call_target="tpu_custom_call" | custom-call | tf_op jit(solution)/shard_map/last/pallas_call | solution.py:559
  228.1 0.0 copy-start.8
  228.1 0.0 copy-start.2
  228.1 0.0 all-reduce.4.cloned.1.call-update
  228.2 1.0 copy-done.4
  229.2 1.1 copy.32
  230.2 0.0 copy-done.7
  230.3 1.4 copy.33
  231.7 41.2 %all-reduce = (f32[576]{0:T(1024)}, f32[576]{0:T(1024)}) all-reduce(f32[576]{0:T(1024)S(1)} %reduce, f32[576]{0:T(1024)S(1)} %reduce.1), channel_id=1, replica_groups=mesh['seq'=8,'batch'=4] {'seq','batch'}, use_global_device_ids=true, to_apply=%region_1.0 | all-reduce | flops 1152 | bytes 9216 | tf_op jit(solution)/shard_map/psum | solution.py:613
  272.9 122.8 %all-reduce.4.cloned.1.call-done = (bf16[576,960]{1,0:T(8,128)(2,1)}, bf16[576,576]{1,0:T(8,128)(2,1)}, bf16[3,576,1536]{2,1,0:T(8,128)(2,1)}) async-done(((bf16[576,960]{1,0:T(8,128)(2,1)}, bf16[576,576]{1,0:T(8,128)(2,1)}, bf16[3,576,1536]{2,1,0:T(8,128)(2,1)}), (bf16[576,960]{1,0:T(8,128)(2,1)}, bf16[576,576]{1,0:T(8,128)(2,1)}, bf16[3,576,1536]{2,1,0:T(8,128)(2,1)})) %all-reduce.4.cloned.1.call-update) | async-done | bytes 7077904 | tf_op jit(solution)/shard_map/psum | solution.py:612
  395.7 1.4 slice_convert_fusion.1
  397.1 0.1 copy-done.1
  397.2 1.2 slice_convert_fusion
  398.4 7.1 %convert_bitcast_fusion = (f32[1536,576]{0,1:T(8,128)}, f32[576,1536]{1,0:T(8,128)}, f32[576,1536]{1,0:T(8,128)}) fusion(bf16[3,576,1536]{2,1,0:T(8,128)(2,1)} %get-tuple-element.58), kind=kLoop, calls=%fused_computation | loop fusion | flops 2654208 | bytes 15925248 | tf_op jit(solution)/shard_map/convert_element_type | solution.py:627
  405.6 1.0 copy.34
  406.6 1.0 copy.35
  407.6 1.2 convert_element_type.36
  (19 shorter events, 0.1 us)
Async XLA Ops:
  7.2 4.2 %copy-start.6 = (bf16[576,192]{0,1:T(8,128)(2,1)S(1)}, bf16[576,192]{0,1:T(8,128)(2,1)}, u32[]{:S(2)}) copy-start(bf16[576,192]{0,1:T(8,128)(2,1)} %param.19) | copy-start | bytes 663556
  7.2 5.0 %copy-start.9 = (bf16[576]{0:T(1024)(128)(2,1)S(1)}, bf16[576]{0:T(1024)(128)(2,1)}, u32[]{:S(2)}) copy-start(bf16[576]{0:T(1024)(128)(2,1)} %param.16) | copy-start | bytes 3460
  7.2 5.6 %copy-start = (bf16[1536,576]{0,1:T(8,128)(2,1)S(1)}, bf16[1536,576]{0,1:T(8,128)(2,1)}, u32[]{:S(2)}) copy-start(bf16[1536,576]{0,1:T(8,128)(2,1)} %param.24) | copy-start | bytes 5308420
  7.2 214.5 %reduce-scatter.2.cloned.1.call-start = ((), (), s32[]{:S(2)}) async-start(), calls=%async_computation.1 | async-start | bytes 3538944 | tf_op jit(solution)/shard_map/reduce_scatter | solution.py:608
  12.8 2.3 copy-start.5
  12.8 3.3 copy-start.10
  78.3 317.5 %all-reduce.4.cloned.1.call-start = ((), (), s32[]{:S(2)}) async-start(), calls=%async_computation.2 | async-start | bytes 14450688 | tf_op jit(solution)/shard_map/psum | solution.py:612
  228.1 1.1 copy-start.4
  228.1 2.1 copy-start.7
  228.1 2.2 copy-start.8
  228.1 2.2 copy-start.2
  395.7 1.5 copy-start.1
  405.6 2.0 copy-start.3
Sparse Core Ops, SparseCore 0:
  78.4 143.2 reduce-scatter.1
  228.4 167.2 all-reduce.3

commit v2 on v1

--- a/solution.py
+++ b/solution.py
@@ -14,6 +14,10 @@
 GROUP = H // KVH
 PAIR = 2 * HD
 META = 16
+LANES = 128
+TILES = 4
+EXTRA = 64
+SPACING = 2
 
 epsilon = 1e-05
 theta_base = 10000.0
@@ -338,7 +342,7 @@
     w_down_ref,
     out_ref,
     grads_ref,
-    grad_out_ref,
+    rest_ref,
     gain_grad_ref,
     d_middle_ref,
     dot_ref,
@@ -359,6 +363,12 @@
     cot_t = cot.T
     result = middle
     d_normed = jnp.zeros((rows, width), f32)
+
+    def put_tiles(first, grad):
+        for tile in range(grad.shape[1] // LANES):
+            part = grad[:, tile * LANES : (tile + 1) * LANES]
+            grads_ref[first // LANES + tile] = part.astype(bf16)
+
     for first in range(0, hidden_units, chunk):
         part = slice(first, first + chunk)
         gate = dot(normed, w_gate_ref[:, part], 1, 0)
@@ -372,9 +382,9 @@
         result = result + dot(hidden, w_down_ref[part, :], 1, 0)
         d_normed = d_normed + dot(d_gate, w_gate_ref[:, part], 1, 1)
         d_normed = d_normed + dot(d_up, w_up_ref[:, part], 1, 1)
-        grads_ref[0, :, part] = dot(normed_t, d_gate, 1, 0).astype(bf16)
-        grads_ref[1, :, part] = dot(normed_t, d_up, 1, 0).astype(bf16)
-        grads_ref[2, :, part] = dot(cot_t, hidden, 1, 0).astype(bf16)
+        put_tiles(first, dot(normed_t, d_gate, 1, 0))
+        put_tiles(hidden_units + first, dot(normed_t, d_up, 1, 0))
+        put_tiles(2 * hidden_units + first, dot(cot_t, hidden, 1, 0))
     out_ref[...] = result.astype(bf16)
     gain_grad_ref[...] = jnp.sum(d_normed * scaled, axis=0, keepdims=True)
     mixed = d_normed * gain
@@ -383,7 +393,12 @@
     )
     d_middle_ref[...] = d_middle
     d_branch = d_middle.astype(bf16)
-    grad_out_ref[...] = dot(att_ref[...].astype(bf16), d_branch, 1, 0).astype(bf16)
+    whole = width // LANES * LANES
+    attended_t = att_ref[...].astype(bf16)
+    put_tiles(3 * hidden_units, dot(attended_t, d_branch[:, :whole], 1, 0))
+    rest = dot(attended_t, d_branch[:, width - LANES :], 1, 0)
+    lane = lax.broadcasted_iota(jnp.int32, rest.shape, 1)
+    rest_ref[...] = jnp.where(lane >= LANES - (width - whole), rest, 0.0).astype(bf16)
     d_attended = dot(w_out_ref[...], d_branch, 1, 1).astype(bf16)
     for head in range(H):
         part = slice(head * HD, (head + 1) * HD)
@@ -403,8 +418,10 @@
         mlp_kernel,
         out_shape=(
             jax.ShapeDtypeStruct((rows, width), bf16),
-            jax.ShapeDtypeStruct((3, width, hidden_units), bf16),
-            jax.ShapeDtypeStruct((H * HD, width), bf16),
+            jax.ShapeDtypeStruct(
+                ((3 * hidden_units + width) // LANES, width, LANES), bf16
+            ),
+            jax.ShapeDtypeStruct((width, LANES), bf16),
             jax.ShapeDtypeStruct((1, width), f32),
             jax.ShapeDtypeStruct((rows, width), f32),
             jax.ShapeDtypeStruct((H, PAIR, rows), bf16),
@@ -417,26 +434,293 @@
     )(tokens, cot, att, w_out, gain, w_gate, w_up, w_down)
 
 
+class Reduction:
+    def __init__(self, refs, sems, height, rank, row):
+        self.source, self.result, self.half, self.from_core, self.from_xy, self.from_z = refs
+        self.send, self.recv = sems
+        self.height = height
+        self.z, self.x = lax.div(rank, 2), lax.rem(rank, 2)
+        self.y, self.core = lax.div(row, 2), lax.rem(row, 2)
+        self.core_mate = (rank, row + 1 - 2 * self.core)
+        self.y_mate = (rank, row + 2 - 4 * self.y)
+        self.x_mate = (rank + 1 - 2 * self.x, row)
+        self.row = row
+        self.split = TILES // 2
+        half, quarter = height // 2, height // 4
+        self.first_a, self.first_b = half * self.x, half * self.y
+        self.other_a, self.other_b = half - self.first_a, half - self.first_b
+        self.quarter_a = self.first_a + quarter * self.y
+        self.quarter_b = self.first_b + quarter * self.x
+        self.across_a = self.first_a + quarter * (1 - self.y)
+        self.across_b = self.first_b + quarter * (1 - self.x)
+
+    def copy(self, src, dst, number, phase, slot, there, target):
+        return pltpu.make_async_remote_copy(
+            src_ref=src,
+            dst_ref=dst,
+            send_sem=self.send.at[number, phase, slot],
+            recv_sem=self.recv.at[number, phase, there],
+            device_id=target,
+            device_id_type=MESH,
+        )
+
+    def rows(self, first, parts):
+        return pl.ds(pl.multiple_of(first, 16), self.height // parts)
+
+    def tiles(self, number, core):
+        return pl.ds(number * 2 * TILES + core * TILES, TILES)
+
+    def quarter_of(self, tile):
+        return jnp.where(tile < self.split, self.quarter_a, self.quarter_b)
+
+    def copies(self, number, phase):
+        head, tail = pl.ds(0, self.split), pl.ds(self.split, TILES - self.split)
+        base = number * 2 * TILES + self.core * TILES
+        out_head = pl.ds(base, self.split)
+        out_tail = pl.ds(base + self.split, TILES - self.split)
+        if phase == 0:
+            src = self.source.at[self.tiles(number, 1 - self.core)]
+            dst = self.from_core.at[number]
+            return [self.copy(src, dst, number, 0, 0, 0, self.core_mate)]
+        if phase in (1, 2):
+            parts = 2 * phase
+            row_a = self.rows(self.other_a if phase == 1 else self.across_a, parts)
+            row_b = self.rows(self.other_b if phase == 1 else self.across_b, parts)
+            size = self.height // parts
+            first = 0 if phase == 1 else self.height // 2
+            mates = (self.x_mate, self.y_mate) if phase == 1 else (self.y_mate, self.x_mate)
+            return [
+                self.copy(
+                    self.half.at[number, part, row],
+                    self.from_xy.at[number, part, pl.ds(first, size)],
+                    number,
+                    phase,
+                    slot,
+                    slot,
+                    mates[slot],
+                )
+                for slot, (part, row) in enumerate(((head, row_a), (tail, row_b)))
+            ]
+        if phase in (3, 4):
+            made = []
+            for step in range(1, TILES):
+                other = lax.rem(self.z + step, TILES)
+                target = (2 * other + self.x, self.row)
+                if phase == 3:
+                    src = self.half.at[number, other, self.rows(self.quarter_of(other), 4)]
+                    dst = self.from_z.at[number, self.z]
+                else:
+                    src = self.result.at[base + self.z, self.rows(self.quarter_of(self.z), 4)]
+                    dst = src
+                made.append(self.copy(src, dst, number, phase, other, self.z, target))
+            return made
+        if phase in (5, 6):
+            parts = 4 if phase == 5 else 2
+            row_a = self.rows(self.quarter_a if phase == 5 else self.first_a, parts)
+            row_b = self.rows(self.quarter_b if phase == 5 else self.first_b, parts)
+            mates = (self.y_mate, self.x_mate) if phase == 5 else (self.x_mate, self.y_mate)
+            return [
+                self.copy(
+                    self.result.at[part, row],
+                    self.result.at[part, row],
+                    number,
+                    phase,
+                    slot,
+                    slot,
+                    mates[slot],
+                )
+                for slot, (part, row) in enumerate(((out_head, row_a), (out_tail, row_b)))
+            ]
+        place = self.result.at[self.tiles(number, self.core)]
+        return [self.copy(place, place, number, 7, 0, 0, self.core_mate)]
+
+    def arrivals(self, number, phase):
+        if phase not in (3, 4):
+            return self.copies(number, phase)
+        made = []
+        base = number * 2 * TILES + self.core * TILES
+        for step in range(1, TILES):
+            other = lax.rem(self.z + step, TILES)
+            target = (2 * other + self.x, self.row)
+            if phase == 3:
+                dst = self.from_z.at[number, other]
+            else:
+                dst = self.result.at[base + other, self.rows(self.quarter_of(other), 4)]
+            made.append(self.copy(dst, dst, number, phase, other, other, target))
+        return made
+
+    def start(self, number, phase):
+        for made in self.copies(number, phase):
+            made.start()
+
+    def finish(self, number, phase):
+        for made in self.arrivals(number, phase):
+            made.wait_recv()
+        head, tail = pl.ds(0, self.split), pl.ds(self.split, TILES - self.split)
+        if phase == 0:
+            own = self.source[self.tiles(number, self.core)].astype(f32)
+            self.half[number] = (own + self.from_core[number].astype(f32)).astype(bf16)
+        if phase in (1, 2):
+            parts = 2 * phase
+            size = self.height // parts
+            first = 0 if phase == 1 else self.height // 2
+            row_a = self.rows(self.first_a if phase == 1 else self.quarter_a, parts)
+            row_b = self.rows(self.first_b if phase == 1 else self.quarter_b, parts)
+            for part, row in ((head, row_a), (tail, row_b)):
+                other = self.from_xy[number, part, first : first + size].astype(f32)
+                own = self.half[number, part, row].astype(f32)
+                self.half[number, part, row] = (own + other).astype(bf16)
+        if phase == 3:
+            row = self.rows(self.quarter_of(self.z), 4)
+            total = self.half[number, self.z, row].astype(f32)
+            for step in range(1, TILES):
+                other = lax.rem(self.z + step, TILES)
+                total = total + self.from_z[number, other].astype(f32)
+            base = number * 2 * TILES + self.core * TILES
+            self.result[base + self.z, row] = total.astype(bf16)
+
+    def event(self, number, phase):
+        if phase > 0:
+            self.finish(number, phase - 1)
+        if phase < 8:
+            self.start(number, phase)
+
+    def drain(self, number):
+        for phase in range(8):
+            for made in self.copies(number, phase):
+                made.wait_send()
+
+
+def reduction_scratch(numbers, height):
+    dma = pltpu.SemaphoreType.DMA
+    return [
+        pltpu.VMEM((numbers, TILES, height, LANES), bf16),
+        pltpu.VMEM((numbers, TILES, height, LANES), bf16),
+        pltpu.VMEM((numbers, TILES, height * 3 // 4, LANES), bf16),
+        pltpu.VMEM((numbers, TILES, height // 4, LANES), bf16),
+        dma((numbers, 8, TILES)),
+        dma((numbers, 8, TILES)),
+    ]
+
+
 def back_kernel(
     ranks,
+    reduce_here,
+    tokens_ref,
     seg_ref,
-    turn_ref,
+    gain_ref,
+    wq_ref,
+    wk_ref,
+    wv_ref,
+    table_ref,
     qt_ref,
     kv_ref,
     lse_ref,
     dot_ref,
     delta_ref,
+    d_middle_ref,
+    source_ref,
+    rest_ref,
+    gain_mlp_ref,
+    out_ref,
+    grads_ref,
+    late_ref,
+    turn_ref,
+    bias_ref,
+    acc_ref,
+    d_all_ref,
     terms_ref,
-    dq_ref,
-    acc_ref,
+    off_out_ref,
+    off_in_ref,
+    z_out_ref,
+    z_in_ref,
+    turn_sem,
+    off_send,
+    off_recv,
+    z_send,
+    z_recv,
+    *reduction_refs,
 ):
     rank = lax.axis_index("seq")
-    rows = seg_ref.shape[1]
+    row = lax.axis_index("batch")
+    rows, width = tokens_ref.shape
+    levels = ranks // 2
+    depth = lax.div(rank, 2)
+    odd = lax.rem(rank, 2)
+    mate = rank + 1 - 2 * odd
+
+    turn_copy = pltpu.make_async_copy(table_ref.at[rank], turn_ref, turn_sem)
+    turn_copy.start()
+    barrier = pltpu.get_barrier_semaphore()
+    peers = [(mate, row)]
+    for step in range(1, levels):
+        peers.append((2 * lax.rem(depth + step, levels) + odd, row))
+    if reduce_here:
+        core = lax.rem(row, 2)
+        peers.append((rank, row + 1 - 2 * core))
+        peers.append((rank, row + 2 - 4 * lax.div(row, 2)))
+    for peer in peers:
+        pl.semaphore_signal(barrier, inc=1, device_id=peer, device_id_type=MESH)
+    pl.semaphore_wait(barrier, len(peers))
+
+    schedule = {}
+    after_loop = []
+    rounds = 0
+    if reduce_here:
+        early_scratch, late_scratch = reduction_refs[:6], reduction_refs[6:12]
+        late_source = reduction_refs[12]
+        rounds = source_ref.shape[0] // (2 * TILES)
+        early = Reduction(
+            (source_ref, grads_ref) + early_scratch[:4], early_scratch[4:], width, rank, row
+        )
+        last = Reduction(
+            (late_source, late_ref) + late_scratch[:4],
+            late_scratch[4:],
+            width + EXTRA,
+            rank,
+            row,
+        )
+        for number in range(rounds):
+            early.start(number, 0)
+        for diagonal in range(1, rounds + 8):
+            events = [
+                (number, diagonal - number)
+                for number in range(rounds)
+                if 1 <= diagonal - number <= 8
+            ]
+            place = 1 + SPACING * (diagonal - 1)
+            if place < KVH * ranks:
+                schedule[place] = events
+            else:
+                after_loop.append(events)
+    else:
+        late_source = late_ref
+
     seg_row = seg_ref[...]
     in_long = long_row(seg_row)
     acc_ref[...] = jnp.zeros_like(acc_ref)
 
-    def pair_step(block, group, bias, level_of):
+    def off_copy(slot, group):
+        return pltpu.make_async_remote_copy(
+            src_ref=off_out_ref.at[slot, group],
+            dst_ref=off_in_ref.at[slot, group],
+            send_sem=off_send.at[slot, group],
+            recv_sem=off_recv.at[slot, group],
+            device_id=(mate, row),
+            device_id_type=MESH,
+        )
+
+    def z_copy(slot, group):
+        return pltpu.make_async_remote_copy(
+            src_ref=z_out_ref.at[slot, group],
+            dst_ref=z_in_ref.at[slot, group],
+            send_sem=z_send.at[slot, group],
+            recv_sem=z_recv.at[slot, group],
+            device_id=(rank - 2, row),
+            device_id_type=MESH,
+        )
+
+    def pair_step(block, group, masked):
         pair = kv_ref[block, group, :rows, :]
         keys_t = pair.T[:HD]
         heads = range(group * GROUP, (group + 1) * GROUP)
@@ -445,9 +729,12 @@
         results = []
         for spot, head in enumerate(heads):
             scores = dot(pair, qt_ref[head], 1, 0)
-            if bias is not None:
-                scores = scores + bias
-            probs = jnp.exp2(scores - level_of(lse_ref[head : head + 1, :]))
+            level = lse_ref[head : head + 1, :]
+            if masked:
+                scores = scores + bias_ref[...]
+            else:
+                level = jnp.where(in_long, level, never)
+            probs = jnp.exp2(scores - level)
             d_probs = dot(pair, dot_ref[head], 1, 0)
             d_scores = (probs * (d_probs - delta_ref[head : head + 1, :])).astype(bf16)
             total = total + dot(probs.astype(bf16), dot_ref[head], 1, 1)
@@ -455,127 +742,327 @@
             results.append(old[spot] + dot(keys_t, d_scores, 1, 0))
         for spot, head in enumerate(heads):
             acc_ref[head] = results[spot]
-        terms_ref[block, group] = total.astype(bf16)
-
-    def level_off(lse):
-        return jnp.where(in_long, lse, never)
+        slot = lax.div(block, 2)
+        straight = lax.rem(block, 2) == odd
+        low = total.astype(bf16)
+
+        @pl.when(straight)
+        def _():
+            terms_ref[slot, group] = low
+
+        @pl.when(jnp.logical_not(straight))
+        def _():
+            off_out_ref[slot, group] = low
+            off_copy(slot, group).start()
+
+    def combine(time):
+        block = time - (levels - depth)
+        valid = (block >= 0) & (block <= rank) & (lax.rem(block + 2 * levels, 2) == odd)
+        slot = lax.div(jnp.maximum(block, 0), 2)
+        from_mate = valid & (mate > block)
+        from_above = valid & (depth < levels - 1)
+        owner = valid & (block == rank)
+        for group in range(KVH):
+
+            @pl.when(from_mate)
+            def _():
+                off_copy(slot, group).wait_recv()
+
+            @pl.when(from_above)
+            def _():
+                z_copy(slot, group).wait_recv()
+
+            @pl.when(valid)
+            def _():
+                total = terms_ref[slot, group].astype(f32)
+                total = total + jnp.where(from_mate, off_in_ref[slot, group].astype(f32), 0.0)
+                total = total + jnp.where(from_above, z_in_ref[slot, group].astype(f32), 0.0)
+                z_out_ref[slot, group] = total.astype(bf16)
+
+            @pl.when(valid & jnp.logical_not(owner))
+            def _():
+                z_copy(slot, group).start()
 
     def step(block, carry):
-        @pl.when(block == 0)
+        @pl.when((block == 0) & (rank > 0))
         def _():
-            for group in range(KVH):
-                key_bias = first_bias(kv_ref[0, group, rows:, :], rows)
-                pair_step(block, group, key_bias, level_off)
-
-        @pl.when(block != 0)
+            key_bias = first_bias(kv_ref[0, 0, rows:, :], rows)
+            bias_ref[...] = key_bias + jnp.where(in_long, 0.0, masked_value)
+
+        @pl.when(block == rank)
         def _():
-            for group in range(KVH):
-                pair_step(block, group, None, level_off)
-
+            bias_ref[...] = own_bias(seg_row)
+
+        masked = (block == 0) | (block == rank)
+        for group in range(KVH):
+
+            @pl.when(masked)
+            def _():
+                pair_step(block, group, True)
+
+            @pl.when(jnp.logical_not(masked) & (block < rank))
+            def _():
+                pair_step(block, group, False)
+
+            for place, events in schedule.items():
+                if place % KVH == group:
+
+                    @pl.when(block == place // KVH)
+                    def _():
+                        for number, phase in events:
+                            early.event(number, phase)
+
+        combine(block)
         return carry
 
-    lax.fori_loop(0, rank, step, 0)
-    bias = own_bias(seg_row)
-    for group in range(KVH):
-        pair_step(rank, group, bias, lambda lse: lse)
-
-    def clear(block, carry):
-        terms_ref[block] = jnp.zeros((KVH, rows, PAIR), bf16)
-        return carry
-
-    lax.fori_loop(rank + 1, ranks, clear, 0)
+    lax.fori_loop(0, ranks, step, 0)
+    combine(ranks)
+
+    turn_copy.wait()
     cosine = turn_ref[: HD // 2]
     sine = turn_ref[HD // 2 :]
+    q_cols, k_cols = H * HD, KVH * HD
     for head in range(H):
-        part = slice(head * HD, (head + 1) * HD)
-        dq_ref[part, :] = turn_back(acc_ref[head] * HD**-0.5, cosine, sine).astype(bf16)
-
-
-def back(seg_row, turn_table, qt, kv, lse, dot_t, delta, ranks):
-    rows = seg_row.shape[1]
-    vmem = pl.BlockSpec(memory_space=pltpu.VMEM)
-    return pl.pallas_call(
-        functools.partial(back_kernel, ranks),
-        out_shape=(
-            jax.ShapeDtypeStruct((ranks, KVH, rows, PAIR), bf16),
-            jax.ShapeDtypeStruct((H * HD, rows), bf16),
-        ),
-        in_specs=[vmem] * 7,
-        out_specs=(vmem,) * 2,
-        scratch_shapes=[pltpu.VMEM((H, HD, rows), f32)],
-        compiler_params=pltpu.CompilerParams(vmem_limit_bytes=VMEM_LIMIT),
-        name="back",
-    )(seg_row, turn_table, qt, kv, lse, dot_t, delta)
-
-
-def last_kernel(
-    tokens_ref,
-    gain_ref,
-    wq_ref,
-    wk_ref,
-    wv_ref,
-    turn_ref,
-    dq_ref,
-    own_ref,
-    d_middle_ref,
-    out_ref,
-    grads_ref,
-    gain_grad_ref,
-    dk_ref,
-    dv_ref,
-):
-    cosine = turn_ref[: HD // 2]
-    sine = turn_ref[HD // 2 :]
+        turned = turn_back(acc_ref[head] * HD**-0.5, cosine, sine)
+        d_all_ref[head * HD : (head + 1) * HD, :] = turned.astype(bf16)
     for group in range(KVH):
-        part = slice(group * HD, (group + 1) * HD)
-        both = own_ref[group].astype(f32).T
-        dk_ref[part, :] = turn_back(both[:HD] * LN2, cosine, sine).astype(bf16)
-        dv_ref[part, :] = both[HD:].astype(bf16)
+        both = z_out_ref[depth, group].astype(f32).T
+        first = q_cols + group * HD
+        turned = turn_back(both[:HD] * LN2, cosine, sine)
+        d_all_ref[first : first + HD, :] = turned.astype(bf16)
+        d_all_ref[first + k_cols : first + k_cols + HD, :] = both[HD:].astype(bf16)
+    used = q_cols + 2 * k_cols
+    d_all_ref[used:, :] = jnp.zeros((d_all_ref.shape[0] - used, rows), bf16)
     inputs = tokens_ref[...].astype(f32)
     inverse = lax.rsqrt(jnp.mean(inputs * inputs, axis=-1, keepdims=True) + epsilon)
     scaled = inputs * inverse
     gain = gain_ref[...].astype(f32)
     normed_t = (scaled * gain).astype(bf16).T
-    q_cols = H * HD
-    k_cols = KVH * HD
-    grads_ref[:, :q_cols] = dot(normed_t, dq_ref[...], 1, 1).astype(bf16)
-    grads_ref[:, q_cols : q_cols + k_cols] = dot(normed_t, dk_ref[...], 1, 1).astype(bf16)
-    grads_ref[:, q_cols + k_cols :] = dot(normed_t, dv_ref[...], 1, 1).astype(bf16)
     d_normed = (
-        dot(dq_ref[...], wq_ref[...], 0, 1)
-        + dot(dk_ref[...], wk_ref[...], 0, 1)
-        + dot(dv_ref[...], wv_ref[...], 0, 1)
+        dot(d_all_ref[:q_cols], wq_ref[...], 0, 1)
+        + dot(d_all_ref[q_cols : q_cols + k_cols], wk_ref[...], 0, 1)
+        + dot(d_all_ref[q_cols + k_cols : used], wv_ref[...], 0, 1)
     )
-    gain_grad_ref[...] = jnp.sum(d_normed * scaled, axis=0, keepdims=True)
+    gain_attn = jnp.sum(d_normed * scaled, axis=0, keepdims=True)
+    spot = lax.broadcasted_iota(jnp.int32, (EXTRA, LANES), 0)
+    for tile in range(2 * TILES):
+        part = slice(tile * LANES, (tile + 1) * LANES)
+        grad = dot(normed_t, d_all_ref[part], 1, 1)
+        if tile == 2 * TILES - 1:
+            grad = grad + rest_ref[...].astype(f32)
+        late_source[tile, :width, :] = grad.astype(bf16)
+        left = min(width - tile * LANES, LANES)
+        if left > 0:
+            chosen = slice(tile * LANES, tile * LANES + left)
+            pad = jnp.zeros((1, LANES - left), f32)
+            first, second = gain_attn[:, chosen], gain_mlp_ref[:, chosen]
+            if left < LANES:
+                first = jnp.concatenate([first, pad], axis=1)
+                second = jnp.concatenate([second, pad], axis=1)
+            extra = jnp.where(spot == 0, first, jnp.where(spot == 1, second, 0.0))
+        else:
+            extra = jnp.zeros((EXTRA, LANES), f32)
+        late_source[tile, width:, :] = extra.astype(bf16)
+
+    if reduce_here:
+        last.start(0, 0)
     mixed = d_normed * gain
     out_ref[...] = d_middle_ref[...] + inverse * (
         mixed - scaled * jnp.mean(mixed * scaled, axis=-1, keepdims=True)
     )
-
-
-def last(tokens, gain, wq, wk, wv, turn_table, dq, own, d_middle):
+    if reduce_here:
+        for phase in range(1, 9):
+            if after_loop:
+                for number, early_phase in after_loop.pop(0):
+                    early.event(number, early_phase)
+            last.event(0, phase)
+        for events in after_loop:
+            for number, early_phase in events:
+                early.event(number, early_phase)
+        for number in range(rounds):
+            early.drain(number)
+        last.drain(0)
+    else:
+        grads_ref[...] = source_ref[...]
+
+    def sent(block, carry):
+        slot = lax.div(block, 2)
+        straight = lax.rem(block, 2) == odd
+        for group in range(KVH):
+
+            @pl.when(jnp.logical_not(straight))
+            def _():
+                off_copy(slot, group).wait_send()
+
+            @pl.when(straight & (block < rank))
+            def _():
+                z_copy(slot, group).wait_send()
+
+        return carry
+
+    lax.fori_loop(0, rank + 1, sent, 0)
+
+
+def back(
+    ranks,
+    reduce_here,
+    tokens,
+    seg_row,
+    gain,
+    wq,
+    wk,
+    wv,
+    qt,
+    kv,
+    lse,
+    dot_t,
+    delta,
+    d_middle,
+    grads,
+    rest,
+    gain_mlp,
+):
     rows, width = tokens.shape
+    levels = ranks // 2
     vmem = pl.BlockSpec(memory_space=pltpu.VMEM)
+    table = jnp.asarray(angle_table(ranks, rows))
+    dma = pltpu.SemaphoreType.DMA
+    late_shape = (2 * TILES, width + EXTRA, LANES)
+    scratch = [
+        pltpu.VMEM((HD, rows), f32),
+        pltpu.VMEM((rows, rows), f32),
+        pltpu.VMEM((H, HD, rows), f32),
+        pltpu.VMEM((2 * TILES * LANES, rows), bf16),
+    ]
+    scratch += [pltpu.VMEM((levels, KVH, rows, PAIR), bf16)] * 5
+    scratch += [dma(())] + [dma((levels, KVH))] * 4
+    if reduce_here:
+        scratch += reduction_scratch(grads.shape[0] // (2 * TILES), width)
+        scratch += reduction_scratch(1, width + EXTRA)
+        scratch += [pltpu.VMEM(late_shape, bf16)]
     return pl.pallas_call(
-        last_kernel,
+        functools.partial(back_kernel, ranks, reduce_here),
         out_shape=(
             jax.ShapeDtypeStruct((rows, width), f32),
-            jax.ShapeDtypeStruct((width, (H + 2 * KVH) * HD), bf16),
+            jax.ShapeDtypeStruct(grads.shape, bf16),
+            jax.ShapeDtypeStruct(late_shape, bf16),
+        ),
+        in_specs=[vmem] * 6 + [pl.BlockSpec(memory_space=pl.ANY)] + [vmem] * 9,
+        out_specs=(vmem,) * 3,
+        scratch_shapes=scratch,
+        compiler_params=pltpu.CompilerParams(
+            collective_id=1, has_side_effects=True, vmem_limit_bytes=VMEM_LIMIT
+        ),
+        name="back",
+    )(
+        tokens,
+        seg_row,
+        gain,
+        wq,
+        wk,
+        wv,
+        table,
+        qt,
+        kv,
+        lse,
+        dot_t,
+        delta,
+        d_middle,
+        grads,
+        rest,
+        gain_mlp,
+    )
+
+
+def finish_kernel(
+    gate_ref,
+    up_ref,
+    down_ref,
+    grads_ref,
+    late_ref,
+    gain_attn_ref,
+    query_ref,
+    key_ref,
+    value_ref,
+    out_ref,
+    gain_mlp_ref,
+    grad_gate_ref,
+    grad_up_ref,
+    grad_down_ref,
+):
+    width = query_ref.shape[0]
+    grad_gate_ref[...] = gate_ref[0].astype(f32)
+    grad_up_ref[...] = up_ref[0].astype(f32)
+    grad_down_ref[...] = down_ref[0].astype(f32).T
+
+    @pl.when(pl.program_id(0) == 0)
+    def _():
+        late = jnp.concatenate(
+            [late_ref[tile, :width, :].astype(f32) for tile in range(2 * TILES)], axis=1
+        )
+        q_cols, k_cols = H * HD, KVH * HD
+        used = q_cols + 2 * k_cols
+        query_ref[...] = late[:, :q_cols]
+        key_ref[...] = late[:, q_cols : q_cols + k_cols]
+        value_ref[...] = late[:, q_cols + k_cols : used]
+        whole = grads_ref.shape[0]
+        for tile in range(whole):
+            out_ref[:, tile * LANES : (tile + 1) * LANES] = grads_ref[tile].astype(f32)
+        out_ref[:, whole * LANES :] = late[:, used : used + width - whole * LANES]
+        for tile in range(-(-width // LANES)):
+            left = min(width - tile * LANES, LANES)
+            chosen = slice(tile * LANES, tile * LANES + left)
+            gain_attn_ref[:, chosen] = late_ref[tile, width : width + 16, :left].astype(f32)[0:1]
+            gain_mlp_ref[:, chosen] = late_ref[tile, width : width + 16, :left].astype(f32)[1:2]
+
+
+def finish(grads, late, width, hidden_units):
+    vmem = pl.BlockSpec(memory_space=pltpu.VMEM)
+    tiles = hidden_units // LANES
+    whole = width // LANES
+    fixed = lambda shape: pl.BlockSpec(shape, lambda i: (0,) * len(shape))
+    tile_at = lambda base: pl.BlockSpec((1, width, LANES), lambda i: (base + i, 0, 0))
+    k_cols = KVH * HD
+    return pl.pallas_call(
+        finish_kernel,
+        grid=(tiles,),
+        out_shape=(
             jax.ShapeDtypeStruct((1, width), f32),
+            jax.ShapeDtypeStruct((width, H * HD), f32),
+            jax.ShapeDtypeStruct((width, k_cols), f32),
+            jax.ShapeDtypeStruct((width, k_cols), f32),
+            jax.ShapeDtypeStruct((H * HD, width), f32),
+            jax.ShapeDtypeStruct((1, width), f32),
+            jax.ShapeDtypeStruct((width, hidden_units), f32),
+            jax.ShapeDtypeStruct((width, hidden_units), f32),
+            jax.ShapeDtypeStruct((hidden_units, width), f32),
         ),
-        in_specs=[vmem] * 9,
-        out_specs=(vmem,) * 3,
-        scratch_shapes=[
-            pltpu.VMEM((KVH * HD, rows), bf16),
-            pltpu.VMEM((KVH * HD, rows), bf16),
+        in_specs=[
+            tile_at(0),
+            tile_at(tiles),
+            tile_at(2 * tiles),
+            pl.BlockSpec((whole, width, LANES), lambda i: (3 * tiles // whole, 0, 0)),
+            fixed(late.shape),
         ],
+        out_specs=(
+            fixed((1, width)),
+            fixed((width, H * HD)),
+            fixed((width, k_cols)),
+            fixed((width, k_cols)),
+            fixed((H * HD, width)),
+            fixed((1, width)),
+            pl.BlockSpec((width, LANES), lambda i: (0, i)),
+            pl.BlockSpec((width, LANES), lambda i: (0, i)),
+            pl.BlockSpec((LANES, width), lambda i: (i, 0)),
+        ),
         compiler_params=pltpu.CompilerParams(vmem_limit_bytes=VMEM_LIMIT),
-        name="last",
-    )(tokens, gain, wq, wk, wv, turn_table, dq, own, d_middle)
+        name="finish",
+    )(grads, grads, grads, grads, late)
 
 
 def local(
     ranks,
+    batches,
     tokens,
     segment_ids,
     gain_attn,
@@ -590,48 +1077,67 @@
     cotangent,
 ):
     rows, width = tokens.shape[1:]
-    rank = lax.axis_index("seq")
     both_axes = ("seq", "batch")
     gain_first = gain_attn.reshape(1, width)
     gain_second = gain_mlp.reshape(1, width)
     qt, kv, att, lse = attend(
         tokens[0], segment_ids, gain_first, w_query, w_key, w_value, ranks
     )
-    output, grads, grad_out, grad_gain_mlp, d_middle, dot_t, delta = mlp(
+    output, grads, rest, grad_gain_mlp, d_middle, dot_t, delta = mlp(
         tokens[0], cotangent[0], att, w_out, gain_second, w_gate, w_up, w_down
     )
-    grads, grad_out = lax.psum((grads, grad_out), both_axes)
-    turn_table = lax.dynamic_index_in_dim(
-        jnp.asarray(angle_table(ranks, rows)), rank, keepdims=False
+    reduce_here = ranks == 2 * TILES and batches == 4
+    d_inputs, reduced, late = back(
+        ranks,
+        reduce_here,
+        tokens[0],
+        segment_ids,
+        gain_first,
+        w_query,
+        w_key,
+        w_value,
+        qt,
+        kv,
+        lse,
+        dot_t,
+        delta,
+        d_middle,
+        grads if reduce_here else rest[None],
+        rest,
+        grad_gain_mlp,
     )
-    terms, dq = back(segment_ids, turn_table, qt, kv, lse, dot_t, delta, ranks)
-    own = lax.psum_scatter(terms, "seq", scatter_dimension=0, tiled=True)[0]
-    d_inputs, late, grad_gain_attn = last(
-        tokens[0], gain_first, w_query, w_key, w_value, turn_table, dq, own, d_middle
-    )
-    late = lax.psum(late, both_axes)
-    grad_gain_attn, grad_gain_mlp = lax.psum((grad_gain_attn, grad_gain_mlp), both_axes)
-    q_cols = H * HD
-    k_cols = KVH * HD
+    if not reduce_here:
+        reduced, late = lax.psum((grads, late), both_axes)
+    (
+        grad_gain_attn,
+        grad_query,
+        grad_key,
+        grad_value,
+        grad_out,
+        grad_gain_mlp,
+        grad_gate,
+        grad_up,
+        grad_down,
+    ) = finish(reduced, late, width, w_gate.shape[1])
     return (
         output[None],
         d_inputs[None],
         grad_gain_attn[0],
-        late[:, :q_cols].astype(f32),
-        late[:, q_cols : q_cols + k_cols].astype(f32),
-        late[:, q_cols + k_cols :].astype(f32),
-        grad_out.astype(f32),
+        grad_query,
+        grad_key,
+        grad_value,
+        grad_out,
         grad_gain_mlp[0],
-        grads[0].astype(f32),
-        grads[1].astype(f32),
-        grads[2].T.astype(f32),
+        grad_gate,
+        grad_up,
+        grad_down,
     )
 
 
 def solution(mesh):
     split = P("batch", "seq", None)
     return jax.shard_map(
-        functools.partial(local, mesh.shape["seq"]),
+        functools.partial(local, mesh.shape["seq"], mesh.shape["batch"]),
         mesh=mesh,
         in_specs=(split, P("batch", "seq")) + (P(),) * 9 + (split,),
         out_specs=(split, split) + (P(),) * 9,

time: 421 us -> 263 us (0.62)
  waiting for transfers between devices: 266 us -> 0 us
  Pallas kernels: 66.3 us -> 232 us
  blocking collectives: 41.2 us -> 0 us
  between operations: 14.3 us -> 0.9 us
  local copies, waits for them, and re-layouts: 16.7 us -> 26.1 us
  other arithmetic: 11 us -> 2.57 us
    pallas_call x2, Pallas kernels: 26.4 us -> 192 us  [the longest x1 179 us: back(): pl.pallas_call(functools.partial(back_kernel, ranks, reduce_here), out_sh...]
    reduce_scatter x1 -> x0, waiting for transfers between devices: 143 us -> none  [local(): own = lax.psum_scatter(terms, 'seq', scatter_dimension=0, tiled=True)[0]]
    psum x1 -> x0, waiting for transfers between devices: 123 us -> none  [local(): late = lax.psum(late, both_axes)]
    psum x1 -> x0, blocking collectives: 41.2 us -> none  [local(): lax.psum((grad_gain_attn, grad_gain_mlp), both_axes)]
    convert_element_type x4 -> x0, other arithmetic: 10.9 us -> none  [the longest x1 7.14 us: local(): grads[2].T.astype(f32)]
    unnamed x31 -> x14, local copies, waits for them, and re-layouts: 13.9 us -> 23.5 us
  transfers between devices with their start and end apart: 2 -> 0, of which waited for: 2 -> 0; matrix products, arithmetic and copies ran while one was open for 1% -> 0% of each run, Pallas kernels for 0% -> 0%
where the time goes in v2:
time: 263 us; the launch traced here: 262 us
  Pallas kernels  232 us (88%)
  local copies, waits for them, and re-layouts  26.1 us (10%)
    pallas_call x1, Pallas kernels, back(): pl.pallas_call(functools.partial(back_kernel, ranks, reduce_here), out_sh...  179 us
    unnamed x14, local copies, waits for them, and re-layouts  23.5 us
    pallas_call x1, Pallas kernels, attend(): pl.pallas_call(functools.partial(attend_kernel, ranks), out_shape=(jax.Sh...  21.3 us
    pallas_call x1, Pallas kernels, mlp(): pl.pallas_call(mlp_kernel, out_shape=(jax.ShapeDtypeStruct((rows, width),...  18.6 us
    pallas_call x1, Pallas kernels, finish(): pl.pallas_call(finish_kernel, grid=(tiles,), out_shape=(jax.ShapeDtypeStr...  13.4 us

profile of v2, /device:TPU:0, one launch (start us, length us, event | category | flops | bytes accessed | tf_op | source)
XLA Modules:
  0.0 261.8 jit_solution(4407153312754565292)
XLA Ops:
  0.6 0.0 copy-start.1
  0.7 1.3 reshape.28.gain_ref
  2.0 1.3 reshape.29.gain_ref
  3.2 0.0 copy-start
  3.2 1.9 copy.27.wk_ref
  5.2 1.8 copy.28.wv_ref
  7.0 2.1 copy.25
  9.1 0.0 copy-done.1
  9.1 1.1 copy.26
  10.2 0.0 copy-done
  10.2 2.2 copy.29.w_down_ref
  12.5 21.3 %attend.1 = (bf16[9,128,512]{2,1,0:T(8,128)(2,1)}, bf16[8,3,528,128]{3,2,1,0:T(8,128)(2,1)}, f32[576,512]{1,0:T(8,128)}, f32[16,512]{1,0:T(8,128)}) custom-call(bf16[512,576]{1,0:T(8,128)(2,1)} %bitcast.4, s32[1,512]{1,0:T(1,128)} %seg_ref.3, bf16[1,576]{1,0:T(2,128)(2,1)} %reshape.28.gain_ref, bf16[576,576]{1,0:T(8,128)(2,1)} %wq_ref.3, ...), custom_call_target="tpu_custom_call" | custom-call | tf_op jit(solution)/shard_map/attend/pallas_call | solution.py:308
  33.8 18.6 %mlp.1 = (bf16[512,576]{1,0:T(8,128)(2,1)}, bf16[40,576,128]{2,1,0:T(8,128)(2,1)}, bf16[576,128]{1,0:T(8,128)(2,1)}, f32[1,576]{1,0:T(1,128)}, f32[512,576]{1,0:...) custom-call(bf16[512,576]{1,0:T(8,128)(2,1)} %bitcast.5, bf16[512,576]{1,0:T(8,128)(2,1)} %bitcast.7, ...), custom_call_target="tpu_custom_call" | custom-call | tf_op jit(solution)/shard_map/mlp/pallas_call | solution.py:417
  52.4 2.1 copy.32
  54.6 179.0 %back.1 = (f32[512,576]{1,0:T(8,128)}, bf16[40,576,128]{2,1,0:T(8,128)(2,1)}, bf16[8,640,128]{2,1,0:T(8,128)(2,1)}) custom-call(bf16[512,576]{1,0:T(8,128)(2,1)} %bitcast.6, s32[1,512]{1,0:T(1,128)} %seg_ref.3, bf16[1,576]{1,0:T(2,128)(2,1)} %reshape.28.gain_ref, bf16[576,576]{1,0:T(8,128)(2,1)} %wq_ref.3, bf16[576,192]{1,0:T(8,128)(2,1)} %copy.27.wk_ref, ...), custom_call_target="tpu_custom_call" | custom-call | tf_op jit(solution)/shard_map/back/pallas_call | solution.py:943
  233.6 2.7 %copy.33 = f32[1,512,576]{1,2,0:T(8,128)} copy(f32[1,512,576]{2,1,0:T(8,128)} %bitcast.8) | data formatting | bytes 2359296
  236.3 13.4 %finish.1 = (f32[1,576]{1,0:T(1,128)}, f32[576,576]{1,0:T(8,128)}, f32[576,192]{1,0:T(8,128)}, f32[576,192]{1,0:T(8,128)}, f32[576,576]{1,0:T(8,128)}, /*index=5...) custom-call(bf16[40,576,128]{2,1,0:T(8,128)(2,1)} %get-tuple-element.46.gate_ref.up_ref.down_ref.grads, ...), custom_call_target="tpu_custom_call" | custom-call | tf_op jit(solution)/shard_map/finish/pallas_call | solution.py:1026
  249.7 1.3 reduce
  250.9 1.3 reduce.1
  252.2 2.1 copy.34
  254.3 2.1 copy.35
  256.3 5.3 %copy.36 = f32[1536,576]{0,1:T(8,128)} copy(f32[1536,576]{1,0:T(8,128)} %get-tuple-element.67) | data formatting | bytes 7077888
Async XLA Ops:
  0.6 8.5 %copy-start.1 = (bf16[1,512,576]{1,2,0:T(8,128)(2,1)S(1)}, bf16[1,512,576]{1,2,0:T(8,128)(2,1)}, u32[]{:S(2)}) copy-start(bf16[1,512,576]{1,2,0:T(8,128)(2,1)} %param.25) | copy-start | bytes 1769476
  3.2 7.0 %copy-start = (bf16[1536,576]{0,1:T(8,128)(2,1)S(1)}, bf16[1536,576]{0,1:T(8,128)(2,1)}, u32[]{:S(2)}) copy-start(bf16[1536,576]{0,1:T(8,128)(2,1)} %param.24) | copy-start | bytes 5308420

commit v3 on v2

--- a/solution.py
+++ b/solution.py
@@ -18,6 +18,7 @@
 TILES = 4
 EXTRA = 64
 SPACING = 2
+FINISH_STEPS = 4
 
 epsilon = 1e-05
 theta_base = 10000.0
@@ -54,6 +55,17 @@
     return jnp.concatenate(
         [first * cosine - second * sine, second * cosine + first * sine], axis=0
     )
+
+
+def column(vector, rows):
+    wide = jnp.broadcast_to(vector.astype(f32).reshape(1, rows), (128, rows))
+    return wide.T[:, :1]
+
+
+def norm_parts(inputs):
+    mean = jnp.mean(inputs * inputs, axis=0, keepdims=True)
+    inverse = lax.rsqrt(mean + epsilon)
+    return inverse, inputs * inverse
 
 
 def turn_back(vectors, cosine, sine):
@@ -107,7 +119,7 @@
 ):
     rank = lax.axis_index("seq")
     row = lax.axis_index("batch")
-    rows = tokens_ref.shape[0]
+    width, rows = tokens_ref.shape
     depth = lax.div(rank, 2)
     odd = lax.rem(rank, 2)
     mate = rank + 1 - 2 * odd
@@ -148,11 +160,10 @@
             device_id_type=MESH,
         )
 
-    inputs = tokens_ref[...].astype(f32)
-    inverse = lax.rsqrt(jnp.mean(inputs * inputs, axis=-1, keepdims=True) + epsilon)
-    normed = (inputs * inverse * gain_ref[...].astype(f32)).astype(bf16)
-    keys = dot(wk_ref[...], normed, 0, 1)
-    values = dot(wv_ref[...], normed, 0, 1)
+    unused, scaled = norm_parts(tokens_ref[...].astype(f32))
+    normed = (scaled * column(gain_ref[...], width)).astype(bf16)
+    keys = dot(wk_ref[...], normed, 1, 0)
+    values = dot(wv_ref[...], normed, 1, 0)
     seg_row = seg_ref[...]
     start = jnp.sum((seg_row != seg_row[:, rows - 1 :]).astype(f32), axis=1, keepdims=True)
     high = jnp.floor(0.5 * start)
@@ -196,7 +207,7 @@
         def _():
             z_copy(block, group).start()
 
-    queries = dot(wq_ref[...], normed, 0, 1)
+    queries = dot(wq_ref[...], normed, 0, 0)
     for head in range(H):
         part = slice(head * HD, head * HD + HD)
         turned = turn(queries[part], cosine, sine) * (LOG2E / HD**0.5)
@@ -301,7 +312,7 @@
 
 
 def attend(tokens, seg_row, gain, wq, wk, wv, ranks):
-    rows, width = tokens.shape
+    width, rows = tokens.shape
     vmem = pl.BlockSpec(memory_space=pltpu.VMEM)
     table = jnp.asarray(angle_table(ranks, rows))
     dma = pltpu.SemaphoreType.DMA
@@ -348,21 +359,19 @@
     dot_ref,
     delta_ref,
 ):
-    rows, width = tokens_ref.shape
+    width, rows = tokens_ref.shape
     hidden_units = w_gate_ref.shape[1]
     chunk = 512
-    inputs = tokens_ref[...].astype(f32)
-    attended = att_ref[...].astype(bf16).T
-    middle = inputs + dot(attended, w_out_ref[...], 1, 0)
-    inverse = lax.rsqrt(jnp.mean(middle * middle, axis=-1, keepdims=True) + epsilon)
-    scaled = middle * inverse
-    gain = gain_ref[...].astype(f32)
-    normed = (scaled * gain).astype(bf16)
-    normed_t = normed.T
-    cot = cot_ref[...]
-    cot_t = cot.T
+    attended = att_ref[...].astype(bf16)
+    middle = tokens_ref[...].astype(f32) + dot(w_out_ref[...], attended, 0, 0)
+    inverse, scaled = norm_parts(middle)
+    gain = column(gain_ref[...], width)
+    normed_t = (scaled * gain).astype(bf16)
+    normed = normed_t.T
+    cot_t = cot_ref[...]
+    cot = cot_t.T
     result = middle
-    d_normed = jnp.zeros((rows, width), f32)
+    d_normed = jnp.zeros((width, rows), f32)
 
     def put_tiles(first, grad):
         for tile in range(grad.shape[1] // LANES):
@@ -373,33 +382,33 @@
         part = slice(first, first + chunk)
         gate = dot(normed, w_gate_ref[:, part], 1, 0)
         up = dot(normed, w_up_ref[:, part], 1, 0)
-        d_hidden = dot(cot, w_down_ref[part, :], 1, 1)
+        d_hidden = dot(cot, w_down_ref[:, part], 1, 0)
         sigmoid = jax.nn.sigmoid(gate)
         silu = gate * sigmoid
         hidden = (silu * up).astype(bf16)
         d_gate = (d_hidden * up * (sigmoid + silu * (1.0 - sigmoid))).astype(bf16)
         d_up = (d_hidden * silu).astype(bf16)
-        result = result + dot(hidden, w_down_ref[part, :], 1, 0)
-        d_normed = d_normed + dot(d_gate, w_gate_ref[:, part], 1, 1)
-        d_normed = d_normed + dot(d_up, w_up_ref[:, part], 1, 1)
+        result = result + dot(w_down_ref[:, part], hidden, 1, 1)
+        d_normed = d_normed + dot(w_gate_ref[:, part], d_gate, 1, 1)
+        d_normed = d_normed + dot(w_up_ref[:, part], d_up, 1, 1)
         put_tiles(first, dot(normed_t, d_gate, 1, 0))
         put_tiles(hidden_units + first, dot(normed_t, d_up, 1, 0))
         put_tiles(2 * hidden_units + first, dot(cot_t, hidden, 1, 0))
     out_ref[...] = result.astype(bf16)
-    gain_grad_ref[...] = jnp.sum(d_normed * scaled, axis=0, keepdims=True)
+    gain_grad = jnp.sum(d_normed * scaled, axis=1, keepdims=True)
+    gain_grad_ref[...] = jnp.broadcast_to(gain_grad, (width, LANES)).T[:1]
     mixed = d_normed * gain
-    d_middle = cot.astype(f32) + inverse * (
-        mixed - scaled * jnp.mean(mixed * scaled, axis=-1, keepdims=True)
+    d_middle = cot_t.astype(f32) + inverse * (
+        mixed - scaled * jnp.mean(mixed * scaled, axis=0, keepdims=True)
     )
     d_middle_ref[...] = d_middle
     d_branch = d_middle.astype(bf16)
     whole = width // LANES * LANES
-    attended_t = att_ref[...].astype(bf16)
-    put_tiles(3 * hidden_units, dot(attended_t, d_branch[:, :whole], 1, 0))
-    rest = dot(attended_t, d_branch[:, width - LANES :], 1, 0)
+    put_tiles(3 * hidden_units, dot(attended, d_branch[:whole], 1, 1))
+    rest = dot(attended, d_branch[width - LANES :], 1, 1)
     lane = lax.broadcasted_iota(jnp.int32, rest.shape, 1)
     rest_ref[...] = jnp.where(lane >= LANES - (width - whole), rest, 0.0).astype(bf16)
-    d_attended = dot(w_out_ref[...], d_branch, 1, 1).astype(bf16)
+    d_attended = dot(w_out_ref[...], d_branch, 1, 0).astype(bf16)
     for head in range(H):
         part = slice(head * HD, (head + 1) * HD)
         dot_ref[head, :HD, :] = jnp.zeros((HD, rows), bf16)
@@ -411,19 +420,19 @@
 
 
 def mlp(tokens, cot, att, w_out, gain, w_gate, w_up, w_down):
-    rows, width = tokens.shape
+    width, rows = tokens.shape
     hidden_units = w_gate.shape[1]
     vmem = pl.BlockSpec(memory_space=pltpu.VMEM)
     return pl.pallas_call(
         mlp_kernel,
         out_shape=(
-            jax.ShapeDtypeStruct((rows, width), bf16),
+            jax.ShapeDtypeStruct((width, rows), bf16),
             jax.ShapeDtypeStruct(
                 ((3 * hidden_units + width) // LANES, width, LANES), bf16
             ),
             jax.ShapeDtypeStruct((width, LANES), bf16),
             jax.ShapeDtypeStruct((1, width), f32),
-            jax.ShapeDtypeStruct((rows, width), f32),
+            jax.ShapeDtypeStruct((width, rows), f32),
             jax.ShapeDtypeStruct((H, PAIR, rows), bf16),
             jax.ShapeDtypeStruct((16, rows), f32),
         ),
@@ -643,7 +652,7 @@
 ):
     rank = lax.axis_index("seq")
     row = lax.axis_index("batch")
-    rows, width = tokens_ref.shape
+    width, rows = tokens_ref.shape
     levels = ranks // 2
     depth = lax.div(rank, 2)
     odd = lax.rem(rank, 2)
@@ -833,17 +842,16 @@
         d_all_ref[first + k_cols : first + k_cols + HD, :] = both[HD:].astype(bf16)
     used = q_cols + 2 * k_cols
     d_all_ref[used:, :] = jnp.zeros((d_all_ref.shape[0] - used, rows), bf16)
-    inputs = tokens_ref[...].astype(f32)
-    inverse = lax.rsqrt(jnp.mean(inputs * inputs, axis=-1, keepdims=True) + epsilon)
-    scaled = inputs * inverse
-    gain = gain_ref[...].astype(f32)
-    normed_t = (scaled * gain).astype(bf16).T
+    inverse, scaled = norm_parts(tokens_ref[...].astype(f32))
+    gain = column(gain_ref[...], width)
+    normed_t = (scaled * gain).astype(bf16)
     d_normed = (
-        dot(d_all_ref[:q_cols], wq_ref[...], 0, 1)
-        + dot(d_all_ref[q_cols : q_cols + k_cols], wk_ref[...], 0, 1)
-        + dot(d_all_ref[q_cols + k_cols : used], wv_ref[...], 0, 1)
+        dot(wq_ref[...], d_all_ref[:q_cols], 1, 0)
+        + dot(wk_ref[...], d_all_ref[q_cols : q_cols + k_cols], 0, 0)
+        + dot(wv_ref[...], d_all_ref[q_cols + k_cols : used], 0, 0)
     )
-    gain_attn = jnp.sum(d_normed * scaled, axis=0, keepdims=True)
+    gain_attn = jnp.sum(d_normed * scaled, axis=1, keepdims=True)
+    gain_attn = jnp.broadcast_to(gain_attn, (width, LANES)).T[:1]
     spot = lax.broadcasted_iota(jnp.int32, (EXTRA, LANES), 0)
     for tile in range(2 * TILES):
         part = slice(tile * LANES, (tile + 1) * LANES)
@@ -868,7 +876,7 @@
         last.start(0, 0)
     mixed = d_normed * gain
     out_ref[...] = d_middle_ref[...] + inverse * (
-        mixed - scaled * jnp.mean(mixed * scaled, axis=-1, keepdims=True)
+        mixed - scaled * jnp.mean(mixed * scaled, axis=0, keepdims=True)
     )
     if reduce_here:
         for phase in range(1, 9):
@@ -922,7 +930,7 @@
     rest,
     gain_mlp,
 ):
-    rows, width = tokens.shape
+    width, rows = tokens.shape
     levels = ranks // 2
     vmem = pl.BlockSpec(memory_space=pltpu.VMEM)
     table = jnp.asarray(angle_table(ranks, rows))
@@ -943,7 +951,7 @@
     return pl.pallas_call(
         functools.partial(back_kernel, ranks, reduce_here),
         out_shape=(
-            jax.ShapeDtypeStruct((rows, width), f32),
+            jax.ShapeDtypeStruct((width, rows), f32),
             jax.ShapeDtypeStruct(grads.shape, bf16),
             jax.ShapeDtypeStruct(late_shape, bf16),
         ),
@@ -980,6 +988,7 @@
     down_ref,
     grads_ref,
     late_ref,
+    d_inputs_ref,
     gain_attn_ref,
     query_ref,
     key_ref,
@@ -989,11 +998,15 @@
     grad_gate_ref,
     grad_up_ref,
     grad_down_ref,
+    d_tokens_ref,
 ):
     width = query_ref.shape[0]
-    grad_gate_ref[...] = gate_ref[0].astype(f32)
-    grad_up_ref[...] = up_ref[0].astype(f32)
-    grad_down_ref[...] = down_ref[0].astype(f32).T
+    d_tokens_ref[...] = d_inputs_ref[...]
+    for tile in range(gate_ref.shape[0]):
+        part = slice(tile * LANES, (tile + 1) * LANES)
+        grad_gate_ref[:, part] = gate_ref[tile].astype(f32)
+        grad_up_ref[:, part] = up_ref[tile].astype(f32)
+        grad_down_ref[:, part] = down_ref[tile].astype(f32)
 
     @pl.when(pl.program_id(0) == 0)
     def _():
@@ -1003,61 +1016,66 @@
         q_cols, k_cols = H * HD, KVH * HD
         used = q_cols + 2 * k_cols
         query_ref[...] = late[:, :q_cols]
-        key_ref[...] = late[:, q_cols : q_cols + k_cols]
-        value_ref[...] = late[:, q_cols + k_cols : used]
+        key_ref[...] = late[:, q_cols : q_cols + k_cols].T
+        value_ref[...] = late[:, q_cols + k_cols : used].T
         whole = grads_ref.shape[0]
         for tile in range(whole):
             out_ref[:, tile * LANES : (tile + 1) * LANES] = grads_ref[tile].astype(f32)
         out_ref[:, whole * LANES :] = late[:, used : used + width - whole * LANES]
-        for tile in range(-(-width // LANES)):
-            left = min(width - tile * LANES, LANES)
-            chosen = slice(tile * LANES, tile * LANES + left)
-            gain_attn_ref[:, chosen] = late_ref[tile, width : width + 16, :left].astype(f32)[0:1]
-            gain_mlp_ref[:, chosen] = late_ref[tile, width : width + 16, :left].astype(f32)[1:2]
-
-
-def finish(grads, late, width, hidden_units):
-    vmem = pl.BlockSpec(memory_space=pltpu.VMEM)
+        extra = [
+            late_ref[tile, width : width + 16, :].astype(f32)
+            for tile in range(-(-width // LANES))
+        ]
+        extra = jnp.concatenate(extra, axis=1)
+        gain_attn_ref[...] = extra[0, :width]
+        gain_mlp_ref[...] = extra[1, :width]
+
+
+def finish(grads, late, d_inputs, hidden_units):
     tiles = hidden_units // LANES
+    steps = FINISH_STEPS
+    width, rows = d_inputs.shape
+    each = tiles // steps
     whole = width // LANES
     fixed = lambda shape: pl.BlockSpec(shape, lambda i: (0,) * len(shape))
-    tile_at = lambda base: pl.BlockSpec((1, width, LANES), lambda i: (base + i, 0, 0))
+    tile_at = lambda base: pl.BlockSpec((each, width, LANES), lambda i: (base * steps + i, 0, 0))
     k_cols = KVH * HD
     return pl.pallas_call(
         finish_kernel,
-        grid=(tiles,),
+        grid=(steps,),
         out_shape=(
-            jax.ShapeDtypeStruct((1, width), f32),
+            jax.ShapeDtypeStruct((width,), f32),
             jax.ShapeDtypeStruct((width, H * HD), f32),
-            jax.ShapeDtypeStruct((width, k_cols), f32),
-            jax.ShapeDtypeStruct((width, k_cols), f32),
+            jax.ShapeDtypeStruct((k_cols, width), f32),
+            jax.ShapeDtypeStruct((k_cols, width), f32),
             jax.ShapeDtypeStruct((H * HD, width), f32),
-            jax.ShapeDtypeStruct((1, width), f32),
+            jax.ShapeDtypeStruct((width,), f32),
             jax.ShapeDtypeStruct((width, hidden_units), f32),
             jax.ShapeDtypeStruct((width, hidden_units), f32),
-            jax.ShapeDtypeStruct((hidden_units, width), f32),
+            jax.ShapeDtypeStruct((width, hidden_units), f32),
+            jax.ShapeDtypeStruct((width, rows), f32),
         ),
         in_specs=[
             tile_at(0),
-            tile_at(tiles),
-            tile_at(2 * tiles),
+            tile_at(1),
+            tile_at(2),
             pl.BlockSpec((whole, width, LANES), lambda i: (3 * tiles // whole, 0, 0)),
             fixed(late.shape),
+            pl.BlockSpec((width // steps, rows), lambda i: (i, 0)),
         ],
         out_specs=(
-            fixed((1, width)),
+            fixed((width,)),
             fixed((width, H * HD)),
-            fixed((width, k_cols)),
-            fixed((width, k_cols)),
+            fixed((k_cols, width)),
+            fixed((k_cols, width)),
             fixed((H * HD, width)),
-            fixed((1, width)),
-            pl.BlockSpec((width, LANES), lambda i: (0, i)),
-            pl.BlockSpec((width, LANES), lambda i: (0, i)),
-            pl.BlockSpec((LANES, width), lambda i: (i, 0)),
-        ),
+            fixed((width,)),
+        )
+        + (pl.BlockSpec((width, each * LANES), lambda i: (0, i)),) * 3
+        + (pl.BlockSpec((width // steps, rows), lambda i: (i, 0)),),
         compiler_params=pltpu.CompilerParams(vmem_limit_bytes=VMEM_LIMIT),
         name="finish",
-    )(grads, grads, grads, grads, late)
+    )(grads, grads, grads, grads, late, d_inputs)
 
 
 def local(
@@ -1076,26 +1094,25 @@
     w_down,
     cotangent,
 ):
-    rows, width = tokens.shape[1:]
+    tokens_t, cot_t = tokens[0].T, cotangent[0].T
+    w_key_t, w_value_t, w_down_t = w_key.T, w_value.T, w_down.T
     both_axes = ("seq", "batch")
-    gain_first = gain_attn.reshape(1, width)
-    gain_second = gain_mlp.reshape(1, width)
     qt, kv, att, lse = attend(
-        tokens[0], segment_ids, gain_first, w_query, w_key, w_value, ranks
+        tokens_t, segment_ids, gain_attn, w_query, w_key_t, w_value_t, ranks
     )
     output, grads, rest, grad_gain_mlp, d_middle, dot_t, delta = mlp(
-        tokens[0], cotangent[0], att, w_out, gain_second, w_gate, w_up, w_down
+        tokens_t, cot_t, att, w_out, gain_mlp, w_gate, w_up, w_down_t
     )
     reduce_here = ranks == 2 * TILES and batches == 4
     d_inputs, reduced, late = back(
         ranks,
         reduce_here,
-        tokens[0],
+        tokens_t,
         segment_ids,
-        gain_first,
+        gain_attn,
         w_query,
-        w_key,
-        w_value,
+        w_key_t,
+        w_value_t,
         qt,
         kv,
         lse,
@@ -1118,19 +1135,20 @@
         grad_gate,
         grad_up,
         grad_down,
-    ) = finish(reduced, late, width, w_gate.shape[1])
+        d_tokens,
+    ) = finish(reduced, late, d_inputs, w_gate.shape[1])
     return (
-        output[None],
-        d_inputs[None],
-        grad_gain_attn[0],
+        output.T[None],
+        d_tokens.T[None],
+        grad_gain_attn,
         grad_query,
-        grad_key,
-        grad_value,
+        grad_key.T,
+        grad_value.T,
         grad_out,
-        grad_gain_mlp[0],
+        grad_gain_mlp,
         grad_gate,
         grad_up,
-        grad_down,
+        grad_down.T,
     )
 
 

time: 263 us -> 224 us (0.85); the launches traced: 262 us -> 219 us
  local copies, waits for them, and re-layouts: 26.1 us -> 0 us
  Pallas kernels: 232 us -> 218 us
    unnamed x14 -> x0, local copies, waits for them, and re-layouts: 23.5 us -> none
    pallas_call x1, Pallas kernels: 179 us -> 169 us  [back(): pl.pallas_call(functools.partial(back_kernel, ranks, reduce_here), out_sh...]
    pallas_call x2, Pallas kernels: 32 us -> 28.8 us  [the longest x1 18.6 us: mlp(): pl.pallas_call(mlp_kernel, out_shape=(jax.ShapeDtypeStruct((width, rows),...]
where the time goes in v3:
time: 224 us; the launch traced here: 219 us
  Pallas kernels  218 us (97%)
    pallas_call x1, Pallas kernels, back(): pl.pallas_call(functools.partial(back_kernel, ranks, reduce_here), out_sh...  169 us
    pallas_call x1, Pallas kernels, attend(): pl.pallas_call(functools.partial(attend_kernel, ranks), out_shape=(jax.Sh...  20.2 us
    pallas_call x1, Pallas kernels, mlp(): pl.pallas_call(mlp_kernel, out_shape=(jax.ShapeDtypeStruct((width, rows),...  18.6 us
    pallas_call x1, Pallas kernels, finish(): pl.pallas_call(finish_kernel, grid=(steps,), out_shape=(jax.ShapeDtypeStr...  10.2 us

profile of v3, /device:TPU:0, one launch (start us, length us, event | category | flops | bytes accessed | tf_op | source)
XLA Modules:
  0.0 219.2 jit_solution(14315444200130878382)
XLA Ops:
  0.6 20.2 %attend.1 = (bf16[9,128,512]{2,1,0:T(8,128)(2,1)}, bf16[8,3,528,128]{3,2,1,0:T(8,128)(2,1)}, f32[576,512]{1,0:T(8,128)}, f32[16,512]{1,0:T(8,128)}) custom-call(bf16[576,512]{1,0:T(8,128)(2,1)} %bitcast.18, s32[1,512]{1,0:T(1,128)} %seg_ref.3, bf16[576]{0:T(1024)(128)(2,1)} %gain_ref.5, bf16[576,576]{1,0:T(8,128)(2,1)} %wq_ref.3, bf16[192,576]{1,0:T(8,128)(2,1)} %bitcast.22, ...), custom_call_target="tpu_custom_call" | custom-call | tf_op jit(solution)/shard_map/attend/pallas_call | solution.py:319
  20.9 18.6 %mlp.1 = (bf16[576,512]{1,0:T(8,128)(2,1)}, bf16[40,576,128]{2,1,0:T(8,128)(2,1)}, bf16[576,128]{1,0:T(8,128)(2,1)}, f32[1,576]{1,0:T(1,128)}, f32[576,512]{1,0:...) custom-call(bf16[576,512]{1,0:T(8,128)(2,1)} %bitcast.19, bf16[576,512]{1,0:T(8,128)(2,1)} %bitcast.26, ...), custom_call_target="tpu_custom_call" | custom-call | tf_op jit(solution)/shard_map/mlp/pallas_call | solution.py:426
  39.5 169.3 %back.1 = (f32[576,512]{1,0:T(8,128)}, bf16[40,576,128]{2,1,0:T(8,128)(2,1)}, bf16[8,640,128]{2,1,0:T(8,128)(2,1)}) custom-call(bf16[576,512]{1,0:T(8,128)(2,1)} %bitcast.20, s32[1,512]{1,0:T(1,128)} %seg_ref.3, bf16[576]{0:T(1024)(128)(2,1)} %gain_ref.5, bf16[576,576]{1,0:T(8,128)(2,1)} %wq_ref.3, bf16[192,576]{1,0:T(8,128)(2,1)} %bitcast.23, ...), custom_call_target="tpu_custom_call" | custom-call | tf_op jit(solution)/shard_map/back/pallas_call | solution.py:951
  208.8 10.2 %finish.1 = (f32[576]{0:T(1024)}, f32[576,576]{1,0:T(8,128)}, f32[192,576]{1,0:T(8,128)}, f32[192,576]{1,0:T(8,128)}, f32[576,576]{1,0:T(8,128)}, /*index=5*/f32...) custom-call(bf16[40,576,128]{2,1,0:T(8,128)(2,1)} %get-tuple-element.46.gate_ref.up_, ...), custom_call_target="tpu_custom_call" | custom-call | tf_op jit(solution)/shard_map/finish/pallas_call | solution.py:1043
